TPU v7x, 128 devices: a whole 4x4x4 slice. The times are simulated.
128 devices in a mesh: wide: 16 (over z, x_hi, core), narrow: 8 (over y, x_lo).
Axes of the slice: x: 4 (x_hi: 2, x_lo: 2; x = x_hi * 2 + x_lo), y: 4, z: 4, core: 2. Of those that a mesh axis runs over, the one named last changes fastest.
Arguments:
- grav_levels: float32 [4, 512, 256, 128], P(None, 'wide', 'narrow'), may hold values from -6 to 6
- grav_step: float32 [4, 512, 256, 128], P(None, 'wide', 'narrow'), may hold values from -6 to 6
- seis_levels: float32 [4, 512, 256, 128], P(None, None, ('wide', 'narrow')), may hold values from -6 to 6
- seis_step: float32 [4, 512, 256, 128], P(None, None, ('wide', 'narrow')), may hold values from -6 to 6
- unit_labels: int32 [4], replicated, may hold values from 0 to 4
- dens_index: int32 [5], replicated, may hold values from 0 to 7
- vel_index: int32 [5], replicated, may hold values from 0 to 7
- dens_table: float32 [8], replicated, may hold values from 0.5 to 2
- vel_table: float32 [8], replicated, may hold values from 0.5 to 2
Outputs:
- grav_gradient: float32 [4, 512, 256, 128], P(None, 'wide', 'narrow')
- grav_curvature: float32 [4, 512, 256, 128], P(None, 'wide', 'narrow')
- seis_gradient: float32 [4, 512, 256, 128], P(None, None, ('wide', 'narrow'))
- seis_curvature: float32 [4, 512, 256, 128], P(None, None, ('wide', 'narrow'))
All inputs are finite; a program needn't handle non-finite values.
Results may differ from a plain program's by a relative error of at most 0.0003.
Values sent between devices are 32-bit elements; how exact they have to be, the bound alone decides.
A program may use at most 128 MiB of HBM per device.

v0:
```python
import jax
import jax.numpy as jnp
from jax import lax
from jax.sharding import PartitionSpec as P

smooth_width = 1.0


def with_halo(block, sides, width):
    for axis, dim in sides:
        count = lax.axis_size(axis)
        forward = [(i, i + 1) for i in range(count - 1)]
        backward = [(target, source) for source, target in forward]
        low = lax.ppermute(
            lax.slice_in_dim(block, block.shape[dim] - width, None, axis=dim), axis, forward
        )
        high = lax.ppermute(lax.slice_in_dim(block, 0, width, axis=dim), axis, backward)
        block = jnp.concatenate([low, block, high], axis=dim)
    return block


def lookup_coeffs(unit_labels, table_index, values_table):
    table_slots = jnp.arange(values_table.shape[0], dtype=jnp.int32)
    per_unit = jnp.sum(
        jnp.where(table_index[:, None] == table_slots[None, :], values_table[None, :], 0.0), axis=1
    )
    unit_slots = jnp.arange(table_index.shape[0], dtype=jnp.int32)
    return jnp.sum(
        jnp.where(unit_labels[:, None] == unit_slots[None, :], per_unit[None, :], 0.0), axis=1
    )


def heaviside(level_field):
    return 0.5 * (1.0 + jnp.tanh(level_field / smooth_width))


def heaviside_slope(level_field):
    tanh_value = jnp.tanh(level_field / smooth_width)
    return 0.5 / smooth_width * (1.0 - tanh_value * tanh_value)


def mix_levels(levels, coeffs):
    summed = coeffs[0] * heaviside(levels[0])
    for level in range(1, levels.shape[0]):
        summed = summed + coeffs[level] * heaviside(levels[level])
    return summed


def mix_steps(levels, directions, coeffs):
    summed = coeffs[0] * heaviside_slope(levels[0]) * directions[0]
    for level in range(1, levels.shape[0]):
        summed = summed + coeffs[level] * heaviside_slope(levels[level]) * directions[level]
    return summed


def chain_rule(levels, coeffs, force):
    return jnp.stack(
        [coeffs[level] * heaviside_slope(levels[level]) * force for level in range(levels.shape[0])]
    )


def cross_product(first_vec, second_vec):
    return (
        first_vec[1] * second_vec[2] - first_vec[2] * second_vec[1],
        first_vec[2] * second_vec[0] - first_vec[0] * second_vec[2],
        first_vec[0] * second_vec[1] - first_vec[1] * second_vec[0],
    )


def inner_gradient(padded):
    depth_pad = jnp.pad(padded, ((0, 0), (0, 0), (1, 1)))
    grad_x = (padded[2:, 1:-1] - padded[:-2, 1:-1]) * 0.5
    grad_y = (padded[1:-1, 2:] - padded[1:-1, :-2]) * 0.5
    grad_z = (depth_pad[1:-1, 1:-1, 2:] - depth_pad[1:-1, 1:-1, :-2]) * 0.5
    return (grad_x, grad_y, grad_z)


def inner_adjoint(vector):
    depth_pad = jnp.pad(vector[2], ((0, 0), (0, 0), (1, 1)))
    along_x = (vector[0][:-2, 1:-1] - vector[0][2:, 1:-1]) * 0.5
    along_y = (vector[1][1:-1, :-2] - vector[1][1:-1, 2:]) * 0.5
    along_z = (depth_pad[1:-1, 1:-1, :-2] - depth_pad[1:-1, 1:-1, 2:]) * 0.5
    return along_x + along_y + along_z


def coupling_vectors(dens_grad, vel_grad, dchange_grad, vchange_grad):
    cross_vec = cross_product(dens_grad, vel_grad)
    change = tuple(
        (
            first_term + second_term
            for first_term, second_term in zip(
                cross_product(dchange_grad, vel_grad), cross_product(dens_grad, vchange_grad)
            )
        )
    )
    return (
        cross_product(vel_grad, cross_vec),
        cross_product(cross_vec, dens_grad),
        cross_product(vel_grad, change),
        cross_product(change, dens_grad),
    )


def to_bricks(stacked):
    row_blocks = lax.all_to_all(
        stacked, ("wide", "narrow"), split_axis=1, concat_axis=2, tiled=True
    )
    return lax.all_to_all(row_blocks, "narrow", split_axis=2, concat_axis=1, tiled=True)


def to_pencils(stacked):
    row_blocks = lax.all_to_all(stacked, "narrow", split_axis=1, concat_axis=2, tiled=True)
    return lax.all_to_all(row_blocks, ("wide", "narrow"), split_axis=2, concat_axis=1, tiled=True)


def coupling(density, velocity, dens_change, vel_change):
    fields = jnp.stack([density, velocity, dens_change, vel_change])
    padded = with_halo(fields, (("wide", 1), ("narrow", 2)), 2)
    gradients = [inner_gradient(padded[number]) for number in range(4)]
    vectors = coupling_vectors(*gradients)
    rows_here = density.shape[0]
    cols_here = density.shape[1]
    row_place = lax.axis_index("wide") * rows_here - 1 + jnp.arange(rows_here + 2, dtype=jnp.int32)
    col_place = (
        lax.axis_index("narrow") * cols_here - 1 + jnp.arange(cols_here + 2, dtype=jnp.int32)
    )
    row_inside = (row_place >= 0) & (row_place < rows_here * lax.axis_size("wide"))
    col_inside = (col_place >= 0) & (col_place < cols_here * lax.axis_size("narrow"))
    inside = row_inside[:, None, None] & col_inside[None, :, None]
    return tuple(
        (
            inner_adjoint(tuple((jnp.where(inside, component, 0.0) for component in vector)))
            for vector in vectors
        )
    )


def shards(
    grav_levels,
    grav_step,
    seis_levels,
    seis_step,
    unit_labels,
    dens_index,
    vel_index,
    dens_table,
    vel_table,
):
    dens_coeff = lookup_coeffs(unit_labels, dens_index, dens_table)
    vel_coeff = lookup_coeffs(unit_labels, vel_index, vel_table)
    density = mix_levels(grav_levels, dens_coeff)
    dens_change = mix_steps(grav_levels, grav_step, dens_coeff)
    moved = to_bricks(
        jnp.stack(
            [mix_levels(seis_levels, vel_coeff), mix_steps(seis_levels, seis_step, vel_coeff)]
        )
    )
    velocity = moved[0]
    vel_change = moved[1]
    dens_force, vel_force, dens_curvature, vel_curvature = coupling(
        density, velocity, dens_change, vel_change
    )
    grav_gradient = chain_rule(grav_levels, dens_coeff, dens_force)
    grav_curvature = chain_rule(grav_levels, dens_coeff, dens_curvature)
    returned = to_pencils(jnp.stack([vel_force, vel_curvature]))
    seis_gradient = chain_rule(seis_levels, vel_coeff, returned[0])
    seis_curvature = chain_rule(seis_levels, vel_coeff, returned[1])
    return (grav_gradient, grav_curvature, seis_gradient, seis_curvature)


def solution(mesh):
    placed = (
        P(None, "wide", "narrow", None),
        P(None, "wide", "narrow", None),
        P(None, None, ("wide", "narrow"), None),
        P(None, None, ("wide", "narrow"), None),
        P(),
        P(),
        P(),
        P(),
        P(),
    )
    return jax.shard_map(
        shards,
        mesh=mesh,
        in_specs=placed,
        out_specs=(
            P(None, "wide", "narrow", None),
            P(None, "wide", "narrow", None),
            P(None, None, ("wide", "narrow"), None),
            P(None, None, ("wide", "narrow"), None),
        ),
        check_vma=False,
    )
```

profile of v0, /device:TPU:1, one launch (start us, length us, event | category | flops | bytes accessed | tf_op | source)
XLA Modules:
  0.0 154.1 jit_solution(7813554918262306020)
XLA Ops:
  6.4 2.5 %fusion.61 = (f32[1,512,2,128]{3,2,1,0:T(2,128)S(1)}, f32[1,512,2,128]{3,2,1,0:T(2,128)S(1)}, f32[1,512,2,128]{3,2,1,0:T(2,128)S(1)}, f32[1,512,2,128]{3,2,1,0:T...) fusion(f32[4,512,2,128]{3,2,1,0:T(2,128)} %param.11, ...), kind=kLoop, calls=%fused_computation.165 | loop fusion | bytes 8388608 | tf_op jit(solution)/shard_map/slice | solution.py:45
  11.1 30.2 %all_to_all.66 = f32[2,512,2,128]{3,2,0,1:T(2,128)S(1)} all-to-all(f32[2,512,2,128]{3,2,0,1:T(2,128)S(1)} %copy.61), channel_id=1, replica_groups=mesh['wide'=16,'narrow'=8] {'wide','narrow'}, dimensions={1} | all-to-all | bytes 2097152 | tf_op jit(solution)/shard_map/all_to_all | solution.py:105
  41.7 1.6 %copy.63 = f32[2,4,256,128]{3,1,0,2:T(4,128)} copy(f32[2,4,256,128]{3,2,1,0:T(8,128)S(1)} %bitcast.91) | data formatting | bytes 2097152 | tf_op jit(solution)/shard_map/all_to_all | solution.py:105
  43.4 4.2 %all-to-all-start.1 = ((f32[2,4,256,128]{3,1,0,2:T(4,128)}), f32[2,4,256,128]{3,1,0,2:T(4,128)}, u32[]{:S(2)}, u32[]{:S(2)}) async-start(f32[2,4,256,128]{3,1,0,2:T(4,128)} %copy.63), calls=%async_computation.1 | async-start | bytes 2097152 | tf_op jit(solution)/shard_map/all_to_all | solution.py:108
  50.2 2.2 %multiply_add_fusion.2 = (f32[1,32,32,128]{3,2,1,0:T(8,128)S(1)}, f32[1,32,32,128]{3,2,1,0:T(8,128)S(1)}) fusion(f32[4,32,32,128]{3,2,1,0:T(8,128)S(1)} %copy-done, f32[]{:T(128)} %bitcast.4, f32[]{:T(128)} %bitcast.3, f32[]{:T(128)} %bitcast.2, f32[]{:T(128)} %bitcast, f32[4,32,32,128]{3,2,1,0:T(8,128)} %param.10), kind=kLoop, calls=%fused_computation.131 | loop fusion | flops 3932160 | bytes 5242896 | tf_op jit(solution)/shard_map/add | solution.py:45
  52.4 9.3 %all-to-all-done.1 = f32[2,4,256,128]{3,1,0,2:T(4,128)} async-done(((f32[2,4,256,128]{3,1,0,2:T(4,128)}), f32[2,4,256,128]{3,1,0,2:T(4,128)}, u32[]{:S(2)}, u32[]{:S(2)}) %all-to-all-start.1) | async-done | bytes 1048608 | tf_op jit(solution)/shard_map/all_to_all | solution.py:108
  61.7 1.4 copy.64
  64.8 5.9 %collective-permute-start = (f32[4,2,32,128]{3,2,1,0:T(8,128)}, f32[4,2,32,128]{3,2,1,0:T(8,128)S(1)}, u32[]{:S(2)}, u32[]{:S(2)}) collective-permute-start(f32[4,2,32,128]{3,2,1,0:T(8,128)} %get-tuple-element.54), channel_id=1, source_target_pairs={{0,8},{8,16},{16,24},{24,32},{32,40},{40,48},{48,56},{56,64},{64,7... | collective-permute-start | bytes 393224 | tf_op jit(solution)/shard_map/ppermute | solution.py:14
  70.7 1.9 %collective-permute-start.1 = (f32[4,2,32,128]{3,2,1,0:T(8,128)S(1)}, f32[4,2,32,128]{3,2,1,0:T(8,128)S(1)}, u32[]{:S(2)}, u32[]{:S(2)}) collective-permute-start(f32[4,2,32,128]{3,2,1,0:T(8,128)S(1)} %get-tuple-element.55), channel_id=1, source_target_pairs={{8,0},{16,8},{24,16},{32,24},{40,32},{48,40},{56,48},{64,56},{72,6... | collective-permute-start | bytes 393224 | tf_op jit(solution)/shard_map/ppermute | solution.py:17
  72.9 5.5 %collective-permute-done.1 = f32[4,2,32,128]{3,2,1,0:T(8,128)S(1)} collective-permute-done((f32[4,2,32,128]{3,2,1,0:T(8,128)S(1)}, f32[4,2,32,128]{3,2,1,0:T(8,128)S(1)}, u32[]{:S(2)}, u32[]{:S(2)}) %collective-permute-start.1) | collective-permute-done | bytes 131104 | tf_op jit(solution)/shard_map/ppermute | solution.py:17
  79.7 1.8 %collective-permute-start.2 = (f32[4,36,2,128]{3,2,1,0:T(2,128)S(1)}, f32[4,36,2,128]{3,2,1,0:T(2,128)S(1)}, u32[]{:S(2)}, u32[]{:S(2)}) collective-permute-start(f32[4,36,2,128]{3,2,1,0:T(2,128)S(1)} %get-tuple-element.50), channel_id=1, source_target_pairs={{0,1},{1,2},{2,3},{3,4},{4,5},{5,6},{6,7},{8,9},{9,10},{10,11},{11... | collective-permute-start | bytes 442376 | tf_op jit(solution)/shard_map/ppermute | solution.py:14
  83.6 3.8 %collective-permute-done.3 = f32[4,36,2,128]{3,2,1,0:T(2,128)S(1)} collective-permute-done((f32[4,36,2,128]{3,2,1,0:T(2,128)S(1)}, f32[4,36,2,128]{3,2,1,0:T(2,128)S(1)}, u32[]{:S(2)}, u32[]{:S(2)}) %collective-permute-start.3) | collective-permute-done | bytes 147488 | tf_op jit(solution)/shard_map/ppermute | solution.py:17
  90.3 1.5 %subtract_select_fusion.2 = (f32[34,34,128]{2,1,0:T(8,128)S(1)}, f32[34,34,128]{2,1,0:T(8,128)S(1)}, f32[34,34,128]{2,1,0:T(8,128)S(1)}) fusion(f32[34,34,128]{2,1,0:T(8,128)S(1)} %get-tuple-element.24, f32[34,34,128]{2,1,0:T(8,128)S(1)} %get-tuple-element.25, pred[34,34]{1,0:T(8,128)(4,1)S(1)} %broadcast_and_fusion, ...), kind=kLoop, calls=%fused_computation.53 | loop fusion | flops 4439040 | bytes 13003776 | tf_op jit(solution)/shard_map/jit(_where)/select_n | solution.py:132
  91.9 2.3 %subtract_select_fusion.1 = (f32[34,34,128]{2,1,0:T(8,128)S(1)}, f32[34,34,128]{2,1,0:T(8,128)S(1)}, f32[34,34,128]{2,1,0:T(8,128)S(1)}, f32[34,34,128]{2,1,0:T(...) fusion(f32[34,34,128]{2,1,0:T(8,128)S(1)} %get-tuple-element.25, ...), kind=kLoop, calls=%fused_computation.52 | loop fusion | flops 5030912 | bytes 14083072 | tf_op jit(solution)/shard_map/jit(_where)/select_n | solution.py:132
  94.2 1.7 %subtract_select_fusion.3 = (f32[34,34,128]{2,1,0:T(8,128)S(1)}, f32[34,34,128]{2,1,0:T(8,128)S(1)}, f32[34,34,128]{2,1,0:T(8,128)}, f32[34,34,128]{2,1,0:T(8,12...) fusion(f32[34,34,128]{2,1,0:T(8,128)S(1)} %get-tuple-element.20, f32[34,34,128]{2,1,0:T(8,128)S(1)} %get-tuple-element.21, ...), kind=kLoop, calls=%fused_computation.54 | loop fusion | flops 3551232 | bytes 10062980 | tf_op jit(solution)/shard_map/jit(_where)/select_n | solution.py:132
  96.8 20.1 %all_to_all.67 = f32[2,32,32,128]{3,2,0,1:T(8,128)S(1)} all-to-all(f32[2,32,32,128]{3,2,0,1:T(8,128)S(1)} %copy.67), channel_id=1, replica_groups=mesh['wide'=16,'narrow'=8] {'narrow'}, dimensions={1} | all-to-all | bytes 2097152 | tf_op jit(solution)/shard_map/all_to_all | solution.py:112
  117.0 1.6 %copy.70 = f32[2,4,256,128]{3,1,0,2:T(4,128)} copy(f32[2,4,256,128]{3,2,1,0:T(8,128)S(1)} %bitcast.93) | data formatting | bytes 2097152 | tf_op jit(solution)/shard_map/all_to_all | solution.py:112
  118.7 7.2 %all-to-all-start.3 = ((f32[2,4,256,128]{3,1,0,2:T(4,128)}), f32[2,4,256,128]{3,1,0,2:T(4,128)}, u32[]{:S(2)}, u32[]{:S(2)}) async-start(f32[2,4,256,128]{3,1,0,2:T(4,128)} %copy.70), calls=%async_computation.3 | async-start | bytes 2097152 | tf_op jit(solution)/shard_map/all_to_all | solution.py:113
  125.9 1.9 %fusion.44 = (f32[1,32,32,128]{3,2,1,0:T(8,128)S(1)}, f32[32,32,128]{2,1,0:T(8,128)S(1)}) fusion(f32[]{:T(128)} %bitcast, f32[4,32,32,128]{3,2,1,0:T(8,128)S(1)} %copy-done, f32[34,34,128]{2,1,0:T(8,128)} %get-tuple-element.72, f32[34,34,128]{2,1,0:T(8,128)S(1)} %get-tuple-element.74, f32[34,34,128]{2,1,0:T(8,128)S(1)} %get-tuple-element.69), kind=kLoop, calls=%fused_computation.121 | loop fusion | flops 1310720 | bytes 4261892 | tf_op jit(solution)/shard_map/stack | solution.py:57
  128.5 1.5 pad_maximum_fusion.2
  130.4 1.5 pad_maximum_fusion.1
  131.9 12.5 %all-to-all-done.3 = f32[2,4,256,128]{3,1,0,2:T(4,128)} async-done(((f32[2,4,256,128]{3,1,0,2:T(4,128)}), f32[2,4,256,128]{3,1,0,2:T(4,128)}, u32[]{:S(2)}, u32[]{:S(2)}) %all-to-all-start.3) | async-done | bytes 1048608 | tf_op jit(solution)/shard_map/all_to_all | solution.py:113
  148.1 2.9 %copy.75 = f32[4,512,2,128]{3,2,1,0:T(2,128)} copy(f32[4,512,2,128]{3,1,2,0:T(8,128)S(1)} %pad_maximum_fusion.4) | data formatting | bytes 4194304
  151.1 2.9 %copy.74 = f32[4,512,2,128]{3,2,1,0:T(2,128)} copy(f32[4,512,2,128]{3,1,2,0:T(8,128)S(1)} %pad_maximum_fusion.3) | data formatting | bytes 4194304
  (67 shorter events, 19.6 us)
Async XLA Ops:
  8.9 0.8 copy-start.5
  8.9 1.0 copy-start.7
  8.9 1.1 copy-start.9
  8.9 1.3 copy-start.11
  41.7 8.5 %copy-start = (f32[4,32,32,128]{3,2,1,0:T(8,128)S(1)}, f32[4,32,32,128]{3,2,1,0:T(8,128)}, u32[]{:S(2)}) copy-start(f32[4,32,32,128]{3,2,1,0:T(8,128)} %param.9) | copy-start | bytes 6291460
  43.4 18.4 %all-to-all-start.1 = ((f32[2,4,256,128]{3,1,0,2:T(4,128)}), f32[2,4,256,128]{3,1,0,2:T(4,128)}, u32[]{:S(2)}, u32[]{:S(2)}) async-start(f32[2,4,256,128]{3,1,0,2:T(4,128)} %copy.63), calls=%async_computation.1 | async-start | bytes 2097152 | tf_op jit(solution)/shard_map/all_to_all | solution.py:108
  63.3 0.8 copy-start.1
  63.3 1.4 copy-start.3
  64.8 8.2 %collective-permute-start = (f32[4,2,32,128]{3,2,1,0:T(8,128)}, f32[4,2,32,128]{3,2,1,0:T(8,128)S(1)}, u32[]{:S(2)}, u32[]{:S(2)}) collective-permute-start(f32[4,2,32,128]{3,2,1,0:T(8,128)} %get-tuple-element.54), channel_id=1, source_target_pairs={{0,8},{8,16},{16,24},{24,32},{32,40},{40,48},{48,56},{56,64},{64,7... | collective-permute-start | bytes 393224 | tf_op jit(solution)/shard_map/ppermute | solution.py:14
  70.7 7.8 %collective-permute-start.1 = (f32[4,2,32,128]{3,2,1,0:T(8,128)S(1)}, f32[4,2,32,128]{3,2,1,0:T(8,128)S(1)}, u32[]{:S(2)}, u32[]{:S(2)}) collective-permute-start(f32[4,2,32,128]{3,2,1,0:T(8,128)S(1)} %get-tuple-element.55), channel_id=1, source_target_pairs={{8,0},{16,8},{24,16},{32,24},{40,32},{48,40},{56,48},{64,56},{72,6... | collective-permute-start | bytes 393224 | tf_op jit(solution)/shard_map/ppermute | solution.py:17
  72.6 14.8 %copy-start.2 = (f32[1,8,4,32,128]{4,3,2,1,0:T(8,128)S(1)}, f32[1,8,4,32,128]{4,3,2,1,0:T(8,128)}, u32[]{:S(2)}) copy-start(f32[1,8,4,32,128]{4,3,2,1,0:T(8,128)} %copy-done.1) | copy-start | bytes 1572868
  72.6 14.8 %copy-start.4 = (f32[1,8,4,32,128]{4,3,2,1,0:T(8,128)S(1)}, f32[1,8,4,32,128]{4,3,2,1,0:T(8,128)}, u32[]{:S(2)}) copy-start(f32[1,8,4,32,128]{4,3,2,1,0:T(8,128)} %copy-done.3) | copy-start | bytes 1572868
  79.7 3.9 %collective-permute-start.2 = (f32[4,36,2,128]{3,2,1,0:T(2,128)S(1)}, f32[4,36,2,128]{3,2,1,0:T(2,128)S(1)}, u32[]{:S(2)}, u32[]{:S(2)}) collective-permute-start(f32[4,36,2,128]{3,2,1,0:T(2,128)S(1)} %get-tuple-element.50), channel_id=1, source_target_pairs={{0,1},{1,2},{2,3},{3,4},{4,5},{5,6},{6,7},{8,9},{9,10},{10,11},{11... | collective-permute-start | bytes 442376 | tf_op jit(solution)/shard_map/ppermute | solution.py:14
  81.5 5.9 %collective-permute-start.3 = (f32[4,36,2,128]{3,2,1,0:T(2,128)S(1)}, f32[4,36,2,128]{3,2,1,0:T(2,128)S(1)}, u32[]{:S(2)}, u32[]{:S(2)}) collective-permute-start(f32[4,36,2,128]{3,2,1,0:T(2,128)S(1)} %get-tuple-element.51), channel_id=1, source_target_pairs={{1,0},{2,1},{3,2},{4,3},{5,4},{6,5},{7,6},{9,8},{10,9},{11,10},{12... | collective-permute-start | bytes 442376 | tf_op jit(solution)/shard_map/ppermute | solution.py:17
  118.7 25.7 %all-to-all-start.3 = ((f32[2,4,256,128]{3,1,0,2:T(4,128)}), f32[2,4,256,128]{3,1,0,2:T(4,128)}, u32[]{:S(2)}, u32[]{:S(2)}) async-start(f32[2,4,256,128]{3,1,0,2:T(4,128)} %copy.70), calls=%async_computation.3 | async-start | bytes 2097152 | tf_op jit(solution)/shard_map/all_to_all | solution.py:113
  125.9 1.9 %copy-start.13 = (f32[34,34,128]{2,1,0:T(8,128)S(1)}, f32[34,34,128]{2,1,0:T(8,128)}, u32[]{:S(2)}) copy-start(f32[34,34,128]{2,1,0:T(8,128)} %get-tuple-element.68) | copy-start | bytes 1775620
  125.9 1.9 %copy-start.14 = (f32[34,34,128]{2,1,0:T(8,128)S(1)}, f32[34,34,128]{2,1,0:T(8,128)}, u32[]{:S(2)}) copy-start(f32[34,34,128]{2,1,0:T(8,128)} %get-tuple-element.75) | copy-start | bytes 1775620
  125.9 1.9 %copy-start.15 = (f32[34,34,128]{2,1,0:T(8,128)S(1)}, f32[34,34,128]{2,1,0:T(8,128)}, u32[]{:S(2)}) copy-start(f32[34,34,128]{2,1,0:T(8,128)} %get-tuple-element.73) | copy-start | bytes 1775620
  145.8 1.0 copy-start.6
  145.8 1.2 copy-start.8
  145.8 1.3 copy-start.10
  145.9 1.5 copy-start.12
where the time goes:
time: 155 us; the launch traced here: 154 us
  blocking collectives  50.3 us (32%)
  waiting for transfers between devices  32.2 us (21%)
  other arithmetic  23.3 us (15%)
  starting transfers between devices  22.4 us (14%)
  local copies, waits for them, and re-layouts  19.7 us (13%)
  between operations  6.14 us (4%)
    all_to_all x1, blocking collectives, to_bricks(): lax.all_to_all(stacked, ('wide', 'narrow'), split_axis=1, concat_axis=2,...  30.2 us
    all_to_all x1, blocking collectives, to_pencils(): lax.all_to_all(stacked, 'narrow', split_axis=1, concat_axis=2, tiled=True)  20.1 us
    all_to_all x1, waiting for transfers between devices, to_pencils(): lax.all_to_all(row_blocks, ('wide', 'narrow'), split_axis=2, concat_axis=...  12.5 us
    ppermute x2, waiting for transfers between devices, with_halo(): lax.ppermute(lax.slice_in_dim(block, 0, width, axis=dim), axis, backward)  9.36 us
    all_to_all x1, waiting for transfers between devices, to_bricks(): lax.all_to_all(row_blocks, 'narrow', split_axis=2, concat_axis=1, tiled=T...  9.34 us
    unnamed x34, local copies, waits for them, and re-layouts  7.98 us
    ppermute x2, starting transfers between devices, with_halo(): lax.ppermute(lax.slice_in_dim(block, block.shape[dim] - width, None, axis...  7.74 us
    all_to_all x1, starting transfers between devices, to_pencils(): lax.all_to_all(row_blocks, ('wide', 'narrow'), split_axis=2, concat_axis=...  7.16 us
  transfers between devices with their start and end apart: 6, of which 6 were waited for; matrix products, arithmetic and copies ran while one was open for 5% of the time, Pallas kernels for 0%

commit v1 on v0

v1 whole, which is shorter than its diff:
```python
import functools

import jax
import jax.numpy as jnp
from jax import lax
from jax.experimental import pallas as pl
from jax.experimental.pallas import tpu as pltpu
from jax.sharding import PartitionSpec as P

MESH = pl.DeviceIdType.MESH
NX = 32
NY = 32
PITCH = NX + 4
MSG = 2 * PITCH
COLS = (NY + 4) * PITCH
PAD = 8


def both(one, other):
    return jnp.logical_and(one, other)


class Place:
    def __init__(self):
        self.w = lax.axis_index("wide")
        self.n = lax.axis_index("narrow")
        self.z = self.w // 4
        self.xh = (self.w // 2) % 2
        self.c = self.w % 2
        self.y = self.n // 2
        self.xl = self.n % 2
        self.x = self.xh * 2 + self.xl
        self.mid = (self.xh + self.xl) % 2

    @staticmethod
    def device(z, xh, c, y, xl):
        return (z * 4 + xh * 2 + c, y * 2 + xl)

    def is_me(self, device):
        return both(device[0] == self.w, device[1] == self.n)

    def across(self, a):
        return self.x + (1 - self.mid) * a * (3 - 2 * self.x)

    def first_leg(self, dz, a, c2):
        z2 = (self.z + dz) % 4
        xr = self.across(a)
        xh2 = self.mid * a + (1 - self.mid) * (xr // 2)
        relay = self.device(z2, xr // 2, self.c, self.y, xr % 2)
        return z2 * 4 + xh2 * 2 + c2, relay, self.z * 4 + a * 2 + c2, self.is_me(relay)

    def second_leg(self, dz, a, c2):
        zs = (self.z + 4 - dz) % 4
        xs = self.across(a)
        xh2 = self.mid * a + (1 - self.mid) * self.xh
        brick = self.device(self.z, xh2, c2, zs, xs // 2)
        return zs * 4 + a * 2 + c2, brick, self.c * 8 + self.y * 2 + xs % 2

    def slab(self, pair):
        return (self.n * 2 + pair // 8, pair % 8)


def coeffs(labels, index, table):
    return [table[index[labels[level]]] for level in range(4)]


def depth_change(field):
    lane = lax.broadcasted_iota(jnp.int32, field.shape, field.ndim - 1)
    up = jnp.where(lane == 127, 0.0, pltpu.roll(field, 127, field.ndim - 1))
    down = jnp.where(lane == 0, 0.0, pltpu.roll(field, 1, field.ndim - 1))
    return up - down


def cross(p, q):
    return (p[1] * q[2] - p[2] * q[1], p[2] * q[0] - p[0] * q[2], p[0] * q[1] - p[1] * q[0])


def cross_first(p, q):
    return p[1] * q[2] - p[2] * q[1]


def coupled(curvature, grads):
    if curvature:
        dens, vel, dchange, vchange = grads
        mixed = tuple(s + t for s, t in zip(cross(dchange, vel), cross(dens, vchange)))
    else:
        dens, vel = grads
        mixed = cross(dens, vel)
    return dens, vel, mixed


def forces_kernel(
    grav_levels,
    grav_step,
    seis_levels,
    seis_step,
    labels,
    dens_index,
    vel_index,
    dens_table,
    vel_table,
    dens_out,
    vel_out,
    gl,
    gs,
    sl,
    st,
    sb,
    hb,
    rb,
    db,
    xs,
    xr,
    q1e,
    q1s,
    q2s,
    acc,
    df,
    rs,
    rv,
    load_sem,
    leg1_send,
    leg1_recv,
    leg2_send,
    leg2_recv,
    xh_send,
    xh_recv,
    yd_send,
    yd_recv,
    yv_send,
    yv_recv,
    ret_send,
    ret_recv,
):
    me = Place()
    slab_rows = seis_levels.shape[1]

    loads = []
    for number, (source, target) in enumerate(
        [
            (seis_levels, sl.at[:, pl.ds(PAD, slab_rows), :]),
            (seis_step, st.at[:, pl.ds(PAD, slab_rows), :]),
            (grav_levels, gl),
            (grav_step, gs),
        ]
    ):
        copy = pltpu.make_async_copy(source, target, load_sem.at[number])
        copy.start()
        loads.append(copy)

    barrier = pltpu.get_barrier_semaphore()

    def greet(device):
        pl.semaphore_signal(barrier, inc=1, device_id=device, device_id_type=MESH)

    def greet_first(i, _):
        device = me.first_leg(i // 2, i % 2, 0)[1]

        @pl.when(jnp.logical_not(me.is_me(device)))
        def _():
            greet(device)

        return 0

    lax.fori_loop(0, 8, greet_first, 0)

    def greet_second(i, _):
        y2, c2, far = i // 4, (i // 2) % 2, i % 2
        xr_mid = 1 + me.xl
        xr_end = 3 * me.xh
        x2 = far * xr_end + (1 - far) * xr_mid
        device = me.device(me.z, x2 // 2, c2, y2, x2 % 2)

        @pl.when(jnp.logical_not(me.is_me(device)))
        def _():
            greet(device)

        return 0

    lax.fori_loop(0, 16, greet_second, 0)

    def greet_return(i, _):
        device = (i, me.z * 2 + me.xh)

        @pl.when(jnp.logical_not(me.is_me(device)))
        def _():
            greet(device)

        return 0

    lax.fori_loop(0, 16, greet_return, 0)
    has_low_x, has_high_x = me.w > 0, me.w < 15
    has_low_y, has_high_y = me.n > 0, me.n < 7
    low_x, high_x = (me.w - 1, me.n), (me.w + 1, me.n)
    low_y, high_y = (me.w, me.n - 1), (me.w, me.n + 1)
    sides = ((has_low_x, low_x), (has_high_x, high_x), (has_low_y, low_y), (has_high_y, high_y))
    for here, device in sides:

        @pl.when(here)
        def _():
            greet(device)

    def not_me(device):
        return 1 - me.is_me(device).astype(jnp.int32)

    expected = 0
    for here, _ in sides:
        expected = expected + here.astype(jnp.int32)
    for i in range(8):
        expected = expected + not_me(me.first_leg(i // 2, i % 2, 0)[1])
    for i in range(16):
        expected = expected + not_me(me.second_leg(i // 4, (i // 2) % 2, i % 2)[1])
        expected = expected + not_me(me.slab(i))

    dens_coeff = [0.5 * v for v in coeffs(labels, dens_index, dens_table)]
    vel_coeff = [0.5 * v for v in coeffs(labels, vel_index, vel_table)]

    def remote(source, target, send, recv, device):
        return pltpu.make_async_remote_copy(
            src_ref=source,
            dst_ref=target,
            send_sem=send,
            recv_sem=recv,
            device_id=device,
            device_id_type=MESH,
        )

    def start_any(source, target, send, recv, device):
        mine = me.is_me(device)

        @pl.when(mine)
        def _():
            pltpu.make_async_copy(source, target, recv).start()

        @pl.when(jnp.logical_not(mine))
        def _():
            remote(source, target, send, recv, device).start()

    def await_send(source, send, device):
        @pl.when(jnp.logical_not(me.is_me(device)))
        def _():
            remote(source, source, send, send, device).wait_send()

    def await_recv(target, recv):
        pltpu.make_async_copy(target, target, recv).wait()

    def message(field, slot):
        return sb.at[field, slot]

    def brick_slot(field, slot):
        return rb.at[field, pl.ds(pl.multiple_of((slot + 1) * MSG, 8), MSG), :]

    def route(i):
        dz, a, c2 = i // 4, (i // 2) % 2, i % 2
        return dz, a, c2

    def leg_two(field, i, source, finish=False):
        dz, a, c2 = route(i)
        slot, brick, there = me.second_leg(dz, a, c2)
        if finish:
            await_send(source, leg2_send.at[field, slot], brick)
        else:
            start_any(
                source,
                brick_slot(field, there),
                leg2_send.at[field, slot],
                leg2_recv.at[field, there],
                brick,
            )

    def send_slabs(field):
        def one(i, _):
            dz, a, c2 = route(i)
            block, relay, slot, stays = me.first_leg(dz, a, c2)
            x_at = block * NX - 2 + lax.broadcasted_iota(jnp.int32, (PITCH, 128), 0)
            inside = both(x_at >= 0, x_at < slab_rows // 2)
            for column in range(2):
                rows = pl.ds(block * 2 * NX + PAD - 4 + column, PITCH, stride=2)
                total = None
                for level in range(4):
                    t = jnp.tanh(sl[level, rows, :])
                    if field == 0:
                        term = vel_coeff[level] * (1.0 + t)
                    else:
                        term = (vel_coeff[level] * (1.0 - t * t)) * st[level, rows, :]
                    total = term if total is None else total + term
                sb[field, block, pl.ds(column * PITCH, PITCH), :] = jnp.where(inside, total, 0.0)

            @pl.when(stays)
            def _():
                leg_two(field, i, message(field, block))

            @pl.when(jnp.logical_not(stays))
            def _():
                remote(
                    message(field, block),
                    hb.at[field, slot],
                    leg1_send.at[field, block],
                    leg1_recv.at[field, slot],
                    relay,
                ).start()

            return 0

        lax.fori_loop(0, 16, one, 0)

    def relay_slabs(field):
        def one(i, _):
            dz, a, c2 = route(i)
            stays = me.first_leg(dz, a, c2)[3]
            slot = me.second_leg(dz, a, c2)[0]

            @pl.when(jnp.logical_not(stays))
            def _():
                await_recv(hb.at[field, slot], leg1_recv.at[field, slot])
                leg_two(field, i, hb.at[field, slot])

            return 0

        lax.fori_loop(0, 16, one, 0)

    loads[0].wait()
    pl.semaphore_wait(barrier, expected)
    send_slabs(0)
    loads[1].wait()
    send_slabs(1)

    loads[2].wait()
    loads[3].wait()

    def dens_row(x):
        dens, change = None, None
        for level in range(4):
            t = jnp.tanh(gl[level, x])
            term = dens_coeff[level] * (1.0 + t)
            slope = (dens_coeff[level] * (1.0 - t * t)) * gs[level, x]
            dens = term if dens is None else dens + term
            change = slope if change is None else change + slope
        rows = pl.ds(2 * PITCH + 2 + x, NY, stride=PITCH)
        db[0, rows, :] = dens
        db[1, rows, :] = change
        return dens, change

    def edge_row(k, _):
        side, row = k // 2, k % 2
        dens, change = dens_row(side * (NX - 2) + row)
        xs[side, pl.ds(pl.multiple_of(row * NY, 8), NY), :] = dens
        xs[side, pl.ds(pl.multiple_of((2 + row) * NY, 8), NY), :] = change
        return 0

    lax.fori_loop(0, 4, edge_row, 0)

    def x_halo(side):
        return remote(
            xs.at[side],
            xr.at[1 - side],
            xh_send.at[side],
            xh_recv.at[1 - side],
            (low_x, high_x)[side],
        )

    for side in range(2):

        @pl.when(sides[side][0])
        def _():
            x_halo(side).start()

    def inner_row(x, _):
        dens_row(x)
        return 0

    lax.fori_loop(2, NX - 2, inner_row, 0)

    relay_slabs(0)

    for side in range(2):
        rows = pl.ds(0, 2 * NY * 2)

        @pl.when(sides[side][0])
        def _():
            await_recv(xr.at[side], xh_recv.at[side])

        @pl.when(jnp.logical_not(sides[side][0]))
        def _():
            xr[side] = jnp.zeros(xr.shape[1:], jnp.float32)

        for field in range(2):
            for row in range(2):
                db[field, pl.ds(2 * PITCH + side * (NX + 2) + row, NY, stride=PITCH), :] = xr[
                    side, pl.ds((field * 2 + row) * NY, NY), :
                ]

    def y_halo(ref, send, recv, field, side):
        source = ref.at[field, pl.ds((2 + side * (NY - 2)) * PITCH, MSG), :]
        target = ref.at[field, pl.ds((1 - side) * (NY + 2) * PITCH, MSG), :]
        return remote(
            source, target, send.at[field, side], recv.at[field, 1 - side], (low_y, high_y)[side]
        )

    def y_halo_start(ref, send, recv, field):
        for side in range(2):

            @pl.when(sides[2 + side][0])
            def _():
                y_halo(ref, send, recv, field, side).start()

            @pl.when(jnp.logical_not(sides[2 + side][0]))
            def _():
                ref[field, pl.ds(side * (NY + 2) * PITCH, MSG), :] = jnp.zeros(
                    (MSG, 128), jnp.float32
                )

    def y_halo_recv(ref, send, recv, field):
        for side in range(2):

            @pl.when(sides[2 + side][0])
            def _():
                await_recv(
                    ref.at[field, pl.ds(side * (NY + 2) * PITCH, MSG), :], recv.at[field, side]
                )

    def y_halo_sent(ref, send, recv, field):
        for side in range(2):

            @pl.when(sides[2 + side][0])
            def _():
                y_halo(ref, send, recv, field, side).wait_send()

    for field in range(2):
        y_halo_start(db, yd_send, yd_recv, field)

    relay_slabs(1)

    def arrive(field):
        for slot in (0, 15):
            await_recv(brick_slot(field, slot), leg2_recv.at[field, slot])
        y_halo_start(rb, yv_send, yv_recv, field)

        def one(slot, _):
            await_recv(brick_slot(field, slot), leg2_recv.at[field, slot])
            return 0

        lax.fori_loop(1, 15, one, 0)

    arrive(0)
    for field in range(2):
        y_halo_recv(db, yd_send, yd_recv, field)
    y_halo_recv(rb, yv_send, yv_recv, 0)

    def gradient(ref, field, yy):
        def at(column, x):
            return ref[field, pl.ds(column * PITCH + 2 + x, NX), :]

        return (
            at(yy, 1) - at(yy, -1),
            at(yy + 1, 0) - at(yy - 1, 0),
            depth_change(at(yy, 0)),
        )

    def edge_gradient(ref, field, x):
        def at(dy, x):
            return ref[field, pl.ds((2 + dy) * PITCH + 2 + x, NY, stride=PITCH), :]

        return (at(0, x + 1) - at(0, x - 1), at(1, x) - at(-1, x), depth_change(at(0, x)))

    def compute(field):
        which = [(db, 0), (rb, 0), (db, 1), (rb, 1)][: 2 + 2 * field]

        for side in range(2):
            x = (-1, NX)[side]
            dens, vel, mixed = coupled(field, [edge_gradient(r, f, x) for r, f in which])
            keep = sides[side][0].astype(jnp.float32)
            q1e[0, side] = cross_first(vel, mixed) * keep
            q1e[1, side] = cross_first(mixed, dens) * keep

        def column(yy):
            dens, vel, mixed = coupled(field, [gradient(r, f, yy) for r, f in which])
            outside = jnp.logical_or(
                both(yy == 1, me.n == 0), both(yy == NY + 2, me.n == 7)
            )
            keep = 1.0 - outside.astype(jnp.float32)
            y = jnp.clip(yy - 2, 0, NY - 1)
            for out, q in enumerate((cross(vel, mixed), cross(mixed, dens))):
                q1s[out, pl.ds(8, NX), :] = q[0]
                q1s[out, pl.ds(7, 1), :] = q1e[out, 0, pl.ds(y, 1), :]
                q1s[out, pl.ds(8 + NX, 1), :] = q1e[out, 1, pl.ds(y, 1), :]
                along_x = q1s[out, pl.ds(7, NX), :] - q1s[out, pl.ds(9, NX), :]
                q2s[out, yy] = q[1] * keep
                acc[out, yy] = along_x - depth_change(q[2])

        column(1)
        column(2)

        def pair(p, _):
            for half in range(2):
                yy = 2 * p + 2 + half
                column(yy + 1)
                df[field, pl.ds(pl.multiple_of((yy - 2) * NX, 8), NX), :] = acc[0, yy] + (
                    q2s[0, yy - 1] - q2s[0, yy + 1]
                )
                rs[field, p, pl.ds(half * NX, NX), :] = acc[1, yy] + (
                    q2s[1, yy - 1] - q2s[1, yy + 1]
                )
            start_any(
                rs.at[field, p],
                rv.at[field, me.w],
                ret_send.at[field, p],
                ret_recv.at[field, me.w],
                me.slab(p),
            )
            return 0

        lax.fori_loop(0, 16, pair, 0)

    compute(0)
    arrive(1)
    y_halo_recv(rb, yv_send, yv_recv, 1)
    compute(1)

    for field in range(2):

        def turn(x, _):
            dens_out[field, x] = df[field, pl.ds(x, NY, stride=NX), :]
            return 0

        lax.fori_loop(0, NX, turn, 0)

    for field in range(2):

        def finish(block, _):
            await_recv(rv.at[field, block], ret_recv.at[field, block])
            for half in range(2):
                vel_out[field, pl.ds(block * 2 * NX + half, NX, stride=2), :] = rv[
                    field, block, pl.ds(half * NX, NX), :
                ]
            return 0

        lax.fori_loop(0, 16, finish, 0)

    for side in range(2):

        @pl.when(sides[side][0])
        def _():
            x_halo(side).wait_send()

    for field in range(2):
        y_halo_sent(db, yd_send, yd_recv, field)
        y_halo_sent(rb, yv_send, yv_recv, field)

        def sent(i, _):
            dz, a, c2 = route(i)
            block, relay, slot, stays = me.first_leg(dz, a, c2)

            @pl.when(jnp.logical_not(stays))
            def _():
                remote(
                    message(field, block),
                    message(field, block),
                    leg1_send.at[field, block],
                    leg1_send.at[field, block],
                    relay,
                ).wait_send()

            leg_two(field, i, hb.at[field, 0], finish=True)
            await_send(rs.at[field, 0], ret_send.at[field, i], me.slab(i))
            return 0

        lax.fori_loop(0, 16, sent, 0)


def chain_kernel(
    labels,
    dens_index,
    vel_index,
    dens_table,
    vel_table,
    grav_levels,
    seis_levels,
    dens_force,
    vel_force,
    grav_gradient,
    grav_curvature,
    seis_gradient,
    seis_curvature,
):
    for levels, force, index, table, outs in (
        (grav_levels, dens_force, dens_index, dens_table, (grav_gradient, grav_curvature)),
        (seis_levels, vel_force, vel_index, vel_table, (seis_gradient, seis_curvature)),
    ):
        scales = [v * (0.5 / 16.0) for v in coeffs(labels, index, table)]
        for level in range(4):
            t = jnp.tanh(levels[level])
            slope = scales[level] * (1.0 - t * t)
            for number in range(2):
                outs[number][level] = slope * force[number]


def shards(
    grav_levels,
    grav_step,
    seis_levels,
    seis_step,
    unit_labels,
    dens_index,
    vel_index,
    dens_table,
    vel_table,
):
    levels, nx, ny, nz = grav_levels.shape
    slab_x, slab_y = seis_levels.shape[1:3]
    rows = slab_x * slab_y
    seis_rows = seis_levels.reshape(levels, rows, nz)
    step_rows = seis_step.reshape(levels, rows, nz)
    tables = (unit_labels, dens_index, vel_index, dens_table, vel_table)
    smem = pl.BlockSpec(memory_space=pltpu.SMEM)
    hbm = pl.BlockSpec(memory_space=pl.ANY)
    vmem = pl.BlockSpec(memory_space=pltpu.VMEM)
    f32 = jnp.float32
    dma = pltpu.SemaphoreType.DMA
    dens_force, vel_force = pl.pallas_call(
        forces_kernel,
        out_shape=(
            jax.ShapeDtypeStruct((2, nx, ny, nz), f32),
            jax.ShapeDtypeStruct((2, rows, nz), f32),
        ),
        in_specs=[hbm] * 4 + [smem] * 5,
        out_specs=(vmem, vmem),
        scratch_shapes=[
            pltpu.VMEM((levels, nx, ny, nz), f32),
            pltpu.VMEM((levels, nx, ny, nz), f32),
            pltpu.VMEM((levels, rows + 4 * PAD, nz), f32),
            pltpu.VMEM((levels, rows + 4 * PAD, nz), f32),
            pltpu.VMEM((2, 16, MSG, nz), f32),
            pltpu.VMEM((2, 16, MSG, nz), f32),
            pltpu.VMEM((2, COLS, nz), f32),
            pltpu.VMEM((2, COLS, nz), f32),
            pltpu.VMEM((2, 4 * NY, nz), f32),
            pltpu.VMEM((2, 4 * NY, nz), f32),
            pltpu.VMEM((2, 2, NY, nz), f32),
            pltpu.VMEM((2, NX + 16, nz), f32),
            pltpu.VMEM((2, NY + 4, NX, nz), f32),
            pltpu.VMEM((2, NY + 4, NX, nz), f32),
            pltpu.VMEM((2, NY * NX, nz), f32),
            pltpu.VMEM((2, 16, 2 * NX, nz), f32),
            pltpu.VMEM((2, 16, 2 * NX, nz), f32),
            dma((4,)),
            dma((2, 16)),
            dma((2, 16)),
            dma((2, 16)),
            dma((2, 16)),
            dma((2,)),
            dma((2,)),
            dma((2, 2)),
            dma((2, 2)),
            dma((2, 2)),
            dma((2, 2)),
            dma((2, 16)),
            dma((2, 16)),
        ],
        compiler_params=pltpu.CompilerParams(
            collective_id=0, has_side_effects=True, vmem_limit_bytes=40 << 20
        ),
        name="forces",
    )(grav_levels, grav_step, seis_rows, step_rows, *tables)

    steps = 8
    brick = pl.BlockSpec((levels, nx // steps, ny, nz), lambda i: (0, i, 0, 0))
    slab = pl.BlockSpec((levels, rows // steps, nz), lambda i: (0, i, 0))
    brick_force = pl.BlockSpec((2, nx // steps, ny, nz), lambda i: (0, i, 0, 0))
    slab_force = pl.BlockSpec((2, rows // steps, nz), lambda i: (0, i, 0))
    brick_shape = jax.ShapeDtypeStruct(grav_levels.shape, f32)
    slab_shape = jax.ShapeDtypeStruct(seis_rows.shape, f32)
    outs = pl.pallas_call(
        chain_kernel,
        grid=(steps,),
        out_shape=(brick_shape, brick_shape, slab_shape, slab_shape),
        in_specs=[smem] * 5 + [brick, slab, brick_force, slab_force],
        out_specs=(brick, brick, slab, slab),
        compiler_params=pltpu.CompilerParams(vmem_limit_bytes=32 << 20),
        name="chain",
    )(*tables, grav_levels, seis_rows, dens_force, vel_force)
    return (
        outs[0],
        outs[1],
        outs[2].reshape(seis_levels.shape),
        outs[3].reshape(seis_levels.shape),
    )


def solution(mesh):
    placed = (
        P(None, "wide", "narrow", None),
        P(None, "wide", "narrow", None),
        P(None, None, ("wide", "narrow"), None),
        P(None, None, ("wide", "narrow"), None),
        P(),
        P(),
        P(),
        P(),
        P(),
    )
    return jax.shard_map(
        shards,
        mesh=mesh,
        in_specs=placed,
        out_specs=placed[:4],
        check_vma=False,
    )
```

time: 155 us -> 75 us (0.48)
  the two profiles are of different devices: /device:TPU:1 before, /device:TPU:65 now
where the time goes in v1:
time: 75 us; the launch traced here: 74.2 us
  Pallas kernels  63.9 us (85%)
  local copies, waits for them, and re-layouts  9.63 us (13%)
    pallas_call x1, Pallas kernels, shards(): pl.pallas_call(forces_kernel, out_shape=(jax.ShapeDtypeStruct((2, nx, ny,...  58.4 us
    unnamed x18, local copies, waits for them, and re-layouts  9.63 us
    pallas_call x1, Pallas kernels, shards(): pl.pallas_call(chain_kernel, grid=(steps,), out_shape=(brick_shape, brick...  5.5 us

profile of v1, /device:TPU:65, one launch (start us, length us, event | category | flops | bytes accessed | tf_op | source)
XLA Modules:
  0.0 74.2 jit_solution(4321876492428732194)
XLA Ops:
  0.6 0.0 copy-start
  0.6 1.6 %copy-done = f32[4,32,32,128]{3,2,1,0:T(8,128)S(1)} copy-done((f32[4,32,32,128]{3,2,1,0:T(8,128)S(1)}, f32[4,32,32,128]{3,2,1,0:T(8,128)}, u32[]{:S(2)}) %copy-start) | copy-done | bytes 2097176
  2.2 0.0 copy-start.1
  2.2 1.6 %copy-done.1 = f32[4,512,2,128]{3,2,1,0:T(2,128)S(1)} copy-done((f32[4,512,2,128]{3,2,1,0:T(2,128)S(1)}, f32[4,512,2,128]{3,2,1,0:T(2,128)}, u32[]{:S(2)}) %copy-start.1) | copy-done | bytes 2097176
  3.8 0.0 copy-start.2
  3.8 1.6 %copy-done.2 = f32[4,32,32,128]{3,2,1,0:T(8,128)S(1)} copy-done((f32[4,32,32,128]{3,2,1,0:T(8,128)S(1)}, f32[4,32,32,128]{3,2,1,0:T(8,128)}, u32[]{:S(2)}) %copy-start.2) | copy-done | bytes 2097176
  5.4 0.0 copy-start.3
  5.4 1.6 %copy-done.3 = f32[4,512,2,128]{3,2,1,0:T(2,128)S(1)} copy-done((f32[4,512,2,128]{3,2,1,0:T(2,128)S(1)}, f32[4,512,2,128]{3,2,1,0:T(2,128)}, u32[]{:S(2)}) %copy-start.3) | copy-done | bytes 2097176
  7.0 0.0 copy-start.4
  7.0 0.7 copy-done.4
  7.7 0.0 copy-start.5
  7.7 0.7 copy-done.5
  8.3 0.0 copy-start.6
  8.3 0.7 copy-done.6
  9.0 0.0 copy-start.7
  9.0 0.7 copy-done.7
  9.6 0.0 copy-start.8
  9.6 0.7 copy-done.8
  10.3 58.4 %forces.1 = (f32[2,32,32,128]{3,2,1,0:T(8,128)S(1)}, f32[2,1024,128]{2,1,0:T(8,128)S(1)}) custom-call(f32[4,32,32,128]{3,2,1,0:T(8,128)S(1)} %copy-done, f32[4,32,32,128]{3,2,1,0:T(8,128)S(1)} %copy-done.2, f32[4,1024,128]{2,1,0:T(8,128)S(1)} %bitcast.4, f32[4,1024,128]{2,1,0:T(8,128)S(1)} %bitcast.6, s32[4]{0:T(128)S(1)} %copy-done.4, s32[5]{0:T(128)S(1)} %copy-done.5, ...), custom_call_target="tpu_custom_call" | custom-call | tf_op jit(solution)/shard_map/forces/pallas_call | solution.py:620
  68.7 5.5 %chain.1 = (f32[4,32,32,128]{3,2,1,0:T(8,128)}, f32[4,32,32,128]{3,2,1,0:T(8,128)}, f32[4,1024,128]{2,1,0:T(8,128)}, f32[4,1024,128]{2,1,0:T(8,128)}) custom-call(s32[4]{0:T(128)S(1)} %copy-done.4, s32[5]{0:T(128)S(1)} %copy-done.5, s32[5]{0:T(128)S(1)} %copy-done.6, f32[8]{0:T(128)S(1)} %copy-done.7, f32[8]{0:T(128)S(1)} %copy-done.8, ...), custom_call_target="tpu_custom_call" | custom-call | tf_op jit(solution)/shard_map/chain/pallas_call | solution.py:673
Async XLA Ops:
  0.6 1.6 %copy-start = (f32[4,32,32,128]{3,2,1,0:T(8,128)S(1)}, f32[4,32,32,128]{3,2,1,0:T(8,128)}, u32[]{:S(2)}) copy-start(f32[4,32,32,128]{3,2,1,0:T(8,128)} %grav_levels.3) | copy-start | bytes 6291460
  2.2 1.6 %copy-start.1 = (f32[4,512,2,128]{3,2,1,0:T(2,128)S(1)}, f32[4,512,2,128]{3,2,1,0:T(2,128)}, u32[]{:S(2)}) copy-start(f32[4,512,2,128]{3,2,1,0:T(2,128)} %param.11) | copy-start | bytes 6291460
  3.8 1.6 %copy-start.2 = (f32[4,32,32,128]{3,2,1,0:T(8,128)S(1)}, f32[4,32,32,128]{3,2,1,0:T(8,128)}, u32[]{:S(2)}) copy-start(f32[4,32,32,128]{3,2,1,0:T(8,128)} %grav_step.1) | copy-start | bytes 6291460
  5.4 1.6 %copy-start.3 = (f32[4,512,2,128]{3,2,1,0:T(2,128)S(1)}, f32[4,512,2,128]{3,2,1,0:T(2,128)}, u32[]{:S(2)}) copy-start(f32[4,512,2,128]{3,2,1,0:T(2,128)} %param.12) | copy-start | bytes 6291460
  7.0 0.7 copy-start.4
  7.7 0.7 copy-start.5
  8.3 0.7 copy-start.6
  9.0 0.7 copy-start.7
  9.6 0.7 copy-start.8

commit v2 on v1

--- a/solution.py
+++ b/solution.py
@@ -94,13 +94,20 @@
     grav_step,
     seis_levels,
     seis_step,
+    labels_in,
+    dens_index_in,
+    vel_index_in,
+    dens_table_in,
+    vel_table_in,
+    dens_out,
+    vel_out,
+    grav_slope,
+    seis_slope,
     labels,
     dens_index,
     vel_index,
     dens_table,
     vel_table,
-    dens_out,
-    vel_out,
     gl,
     gs,
     sl,
@@ -138,6 +145,11 @@
     loads = []
     for number, (source, target) in enumerate(
         [
+            (labels_in, labels),
+            (dens_index_in, dens_index),
+            (vel_index_in, vel_index),
+            (dens_table_in, dens_table),
+            (vel_table_in, vel_table),
             (seis_levels, sl.at[:, pl.ds(PAD, slab_rows), :]),
             (seis_step, st.at[:, pl.ds(PAD, slab_rows), :]),
             (grav_levels, gl),
@@ -212,6 +224,8 @@
         expected = expected + not_me(me.second_leg(i // 4, (i // 2) % 2, i % 2)[1])
         expected = expected + not_me(me.slab(i))
 
+    for copy in loads[:5]:
+        copy.wait()
     dens_coeff = [0.5 * v for v in coeffs(labels, dens_index, dens_table)]
     vel_coeff = [0.5 * v for v in coeffs(labels, vel_index, vel_table)]
 
@@ -319,21 +333,23 @@
 
         lax.fori_loop(0, 16, one, 0)
 
-    loads[0].wait()
+    loads[5].wait()
     pl.semaphore_wait(barrier, expected)
     send_slabs(0)
-    loads[1].wait()
+    loads[6].wait()
     send_slabs(1)
 
-    loads[2].wait()
-    loads[3].wait()
+    loads[7].wait()
+    loads[8].wait()
 
     def dens_row(x):
         dens, change = None, None
         for level in range(4):
             t = jnp.tanh(gl[level, x])
             term = dens_coeff[level] * (1.0 + t)
-            slope = (dens_coeff[level] * (1.0 - t * t)) * gs[level, x]
+            slope = dens_coeff[level] * (1.0 - t * t)
+            grav_slope[level, x] = slope * (1.0 / 16.0)
+            slope = slope * gs[level, x]
             dens = term if dens is None else dens + term
             change = slope if change is None else change + slope
         rows = pl.ds(2 * PITCH + 2 + x, NY, stride=PITCH)
@@ -525,6 +541,15 @@
 
         lax.fori_loop(0, NX, turn, 0)
 
+    def seis_rows(i, _):
+        for level in range(4):
+            t = jnp.tanh(sl[level, pl.ds(pl.multiple_of(PAD + i * 32, 8), 32), :])
+            scale = vel_coeff[level] * (1.0 / 16.0)
+            seis_slope[level, pl.ds(pl.multiple_of(i * 32, 8), 32), :] = scale * (1.0 - t * t)
+        return 0
+
+    lax.fori_loop(0, slab_rows // 32, seis_rows, 0)
+
     for field in range(2):
 
         def finish(block, _):
@@ -569,30 +594,26 @@
 
 
 def chain_kernel(
-    labels,
-    dens_index,
-    vel_index,
-    dens_table,
-    vel_table,
-    grav_levels,
-    seis_levels,
+    steps,
     dens_force,
     vel_force,
+    grav_slope,
+    seis_slope,
     grav_gradient,
     grav_curvature,
     seis_gradient,
     seis_curvature,
 ):
-    for levels, force, index, table, outs in (
-        (grav_levels, dens_force, dens_index, dens_table, (grav_gradient, grav_curvature)),
-        (seis_levels, vel_force, vel_index, vel_table, (seis_gradient, seis_curvature)),
+    for slope, force, outs in (
+        (grav_slope, dens_force, (grav_gradient, grav_curvature)),
+        (seis_slope, vel_force, (seis_gradient, seis_curvature)),
     ):
-        scales = [v * (0.5 / 16.0) for v in coeffs(labels, index, table)]
+        rows = slope.shape[1] // steps
+        here = pl.ds(pl.program_id(0) * rows, rows)
         for level in range(4):
-            t = jnp.tanh(levels[level])
-            slope = scales[level] * (1.0 - t * t)
+            factor = slope[level, here]
             for number in range(2):
-                outs[number][level] = slope * force[number]
+                outs[number][level] = factor * force[number, here]
 
 
 def shards(
@@ -612,20 +633,24 @@
     seis_rows = seis_levels.reshape(levels, rows, nz)
     step_rows = seis_step.reshape(levels, rows, nz)
     tables = (unit_labels, dens_index, vel_index, dens_table, vel_table)
-    smem = pl.BlockSpec(memory_space=pltpu.SMEM)
-    hbm = pl.BlockSpec(memory_space=pl.ANY)
+    hbm = pl.BlockSpec(memory_space=pltpu.HBM)
     vmem = pl.BlockSpec(memory_space=pltpu.VMEM)
     f32 = jnp.float32
     dma = pltpu.SemaphoreType.DMA
-    dens_force, vel_force = pl.pallas_call(
+    brick_shape = jax.ShapeDtypeStruct(grav_levels.shape, f32)
+    slab_shape = jax.ShapeDtypeStruct(seis_rows.shape, f32)
+    forces = pl.pallas_call(
         forces_kernel,
         out_shape=(
             jax.ShapeDtypeStruct((2, nx, ny, nz), f32),
             jax.ShapeDtypeStruct((2, rows, nz), f32),
+            brick_shape,
+            slab_shape,
         ),
-        in_specs=[hbm] * 4 + [smem] * 5,
-        out_specs=(vmem, vmem),
+        in_specs=[hbm] * 9,
+        out_specs=(vmem,) * 4,
         scratch_shapes=[
+            *(pltpu.SMEM(table.shape, table.dtype) for table in tables),
             pltpu.VMEM((levels, nx, ny, nz), f32),
             pltpu.VMEM((levels, nx, ny, nz), f32),
             pltpu.VMEM((levels, rows + 4 * PAD, nz), f32),
@@ -643,7 +668,7 @@
             pltpu.VMEM((2, NY * NX, nz), f32),
             pltpu.VMEM((2, 16, 2 * NX, nz), f32),
             pltpu.VMEM((2, 16, 2 * NX, nz), f32),
-            dma((4,)),
+            dma((9,)),
             dma((2, 16)),
             dma((2, 16)),
             dma((2, 16)),
@@ -661,24 +686,20 @@
             collective_id=0, has_side_effects=True, vmem_limit_bytes=40 << 20
         ),
         name="forces",
-    )(grav_levels, grav_step, seis_rows, step_rows, *tables)
+    )(*(pltpu.with_memory_space_constraint(v, pltpu.HBM) for v in (grav_levels, grav_step, seis_rows, step_rows, *tables)))
 
     steps = 8
     brick = pl.BlockSpec((levels, nx // steps, ny, nz), lambda i: (0, i, 0, 0))
     slab = pl.BlockSpec((levels, rows // steps, nz), lambda i: (0, i, 0))
-    brick_force = pl.BlockSpec((2, nx // steps, ny, nz), lambda i: (0, i, 0, 0))
-    slab_force = pl.BlockSpec((2, rows // steps, nz), lambda i: (0, i, 0))
-    brick_shape = jax.ShapeDtypeStruct(grav_levels.shape, f32)
-    slab_shape = jax.ShapeDtypeStruct(seis_rows.shape, f32)
     outs = pl.pallas_call(
-        chain_kernel,
+        functools.partial(chain_kernel, steps),
         grid=(steps,),
         out_shape=(brick_shape, brick_shape, slab_shape, slab_shape),
-        in_specs=[smem] * 5 + [brick, slab, brick_force, slab_force],
+        in_specs=[vmem] * 4,
         out_specs=(brick, brick, slab, slab),
         compiler_params=pltpu.CompilerParams(vmem_limit_bytes=32 << 20),
         name="chain",
-    )(*tables, grav_levels, seis_rows, dens_force, vel_force)
+    )(*forces)
     return (
         outs[0],
         outs[1],

time: 75 us -> 63.2 us (0.84)
  local copies, waits for them, and re-layouts: 9.63 us -> 0 us
  Pallas kernels: 63.9 us -> 61.9 us
    unnamed x18 -> x0, local copies, waits for them, and re-layouts: 9.63 us -> none
    pallas_call x1, Pallas kernels: 5.5 us -> 4.46 us  [shards(): pl.pallas_call(functools.partial(chain_kernel, steps), grid=(steps,), out...]
    pallas_call x1, Pallas kernels: 58.4 us -> 57.4 us  [shards(): pl.pallas_call(forces_kernel, out_shape=(jax.ShapeDtypeStruct((2, nx, ny,...]
where the time goes in v2:
time: 63.2 us; the launch traced here: 62.5 us
  Pallas kernels  61.9 us (98%)
  between operations  0.64 us (1%)
    pallas_call x1, Pallas kernels, shards(): pl.pallas_call(forces_kernel, out_shape=(jax.ShapeDtypeStruct((2, nx, ny,...  57.4 us
    pallas_call x1, Pallas kernels, shards(): pl.pallas_call(functools.partial(chain_kernel, steps), grid=(steps,), out...  4.46 us

profile of v2, /device:TPU:65, one launch (start us, length us, event | category | flops | bytes accessed | tf_op | source)
XLA Modules:
  0.0 62.5 jit_solution(9918355573747520797)
XLA Ops:
  0.6 57.4 %forces.1 = (f32[2,32,32,128]{3,2,1,0:T(8,128)S(1)}, f32[2,1024,128]{2,1,0:T(8,128)S(1)}, f32[4,32,32,128]{3,2,1,0:T(8,128)S(1)}, f32[4,1024,128]{2,1,0:T(8,128)S(1)}) custom-call(f32[4,32,32,128]{3,2,1,0:T(8,128)} %grav_levels.1, f32[4,32,32,128]{3,2,1,0:T(8,128)} %grav_step.1, f32[4,1024,128]{2,1,0:T(8,128)} %bitcast.4, f32[4,1024,128]{2,1,0:T(8,128)} %bitcast.5, ...), custom_call_target="tpu_custom_call" | custom-call | tf_op jit(solution)/shard_map/forces/pallas_call | solution.py:642
  58.1 4.5 %chain.1 = (f32[4,32,32,128]{3,2,1,0:T(8,128)}, f32[4,32,32,128]{3,2,1,0:T(8,128)}, f32[4,1024,128]{2,1,0:T(8,128)}, f32[4,1024,128]{2,1,0:T(8,128)}) custom-call(f32[2,32,32,128]{3,2,1,0:T(8,128)S(1)} %get-tuple-element.12.dens_force, f32[2,1024,128]{2,1,0:T(8,128)S(1)} %get-tuple-element.13.vel_force, f32[4,32,32,128]{3,2,1,0:T(8,128)S(1)} %get-tuple-element.14.grav_slope, ...), custom_call_target="tpu_custom_call" | custom-call | tf_op jit(solution)/shard_map/chain/pallas_call | solution.py:694

commit v3 on v2

--- a/solution.py
+++ b/solution.py
@@ -42,22 +42,35 @@
     def across(self, a):
         return self.x + (1 - self.mid) * a * (3 - 2 * self.x)
 
-    def first_leg(self, dz, a, c2):
-        z2 = (self.z + dz) % 4
+    def step(self, i):
+        pair, half = i // 2, i % 2
+        return pair // 2 + 2 * half, (pair + half) % 2
+
+    def side(self, e):
+        return 1 - e + (1 - self.xh) * self.xl * (2 * e - 1)
+
+    def first_leg(self, i):
+        d, e = self.step(i)
+        a = self.side(e)
+        z2 = (self.z + self.y + d) % 4
         xr = self.across(a)
         xh2 = self.mid * a + (1 - self.mid) * (xr // 2)
-        relay = self.device(z2, xr // 2, self.c, self.y, xr % 2)
-        return z2 * 4 + xh2 * 2 + c2, relay, self.z * 4 + a * 2 + c2, self.is_me(relay)
-
-    def second_leg(self, dz, a, c2):
-        zs = (self.z + 4 - dz) % 4
+        return z2 * 2 + xh2, self.device(z2, xr // 2, self.c, self.y, xr % 2)
+
+    def second_leg(self, i, c2):
+        d, e = self.step(i)
+        a = self.side(e)
+        zs = (self.z + 8 - self.y - d) % 4
         xs = self.across(a)
         xh2 = self.mid * a + (1 - self.mid) * self.xh
         brick = self.device(self.z, xh2, c2, zs, xs // 2)
-        return zs * 4 + a * 2 + c2, brick, self.c * 8 + self.y * 2 + xs % 2
-
-    def slab(self, pair):
-        return (self.n * 2 + pair // 8, pair % 8)
+        return brick, self.c * 8 + self.y * 2 + xs % 2
+
+    def way_back(self, i, c2):
+        d, e = self.step(i)
+        y2 = (self.y + self.z + d) % 4
+        pair = c2 * 8 + y2 * 2 + (self.xh + e) % 2
+        return pair, (self.n * 2 + c2, pair % 8)
 
 
 def coeffs(labels, index, table):
@@ -73,20 +86,6 @@
 
 def cross(p, q):
     return (p[1] * q[2] - p[2] * q[1], p[2] * q[0] - p[0] * q[2], p[0] * q[1] - p[1] * q[0])
-
-
-def cross_first(p, q):
-    return p[1] * q[2] - p[2] * q[1]
-
-
-def coupled(curvature, grads):
-    if curvature:
-        dens, vel, dchange, vchange = grads
-        mixed = tuple(s + t for s, t in zip(cross(dchange, vel), cross(dens, vchange)))
-    else:
-        dens, vel = grads
-        mixed = cross(dens, vel)
-    return dens, vel, mixed
 
 
 def forces_kernel(
@@ -118,6 +117,10 @@
     db,
     xs,
     xr,
+    grads,
+    edge_grads,
+    mixes,
+    edge_mixes,
     q1e,
     q1s,
     q2s,
@@ -165,42 +168,28 @@
     def greet(device):
         pl.semaphore_signal(barrier, inc=1, device_id=device, device_id_type=MESH)
 
-    def greet_first(i, _):
-        device = me.first_leg(i // 2, i % 2, 0)[1]
-
-        @pl.when(jnp.logical_not(me.is_me(device)))
-        def _():
-            greet(device)
-
-        return 0
-
-    lax.fori_loop(0, 8, greet_first, 0)
-
-    def greet_second(i, _):
-        y2, c2, far = i // 4, (i // 2) % 2, i % 2
-        xr_mid = 1 + me.xl
-        xr_end = 3 * me.xh
-        x2 = far * xr_end + (1 - far) * xr_mid
-        device = me.device(me.z, x2 // 2, c2, y2, x2 % 2)
-
-        @pl.when(jnp.logical_not(me.is_me(device)))
-        def _():
-            greet(device)
-
-        return 0
-
-    lax.fori_loop(0, 16, greet_second, 0)
-
-    def greet_return(i, _):
-        device = (i, me.z * 2 + me.xh)
-
-        @pl.when(jnp.logical_not(me.is_me(device)))
-        def _():
-            greet(device)
-
-        return 0
-
-    lax.fori_loop(0, 16, greet_return, 0)
+    for dz in range(1, 4):
+        greet(me.device((me.z + dz) % 4, me.xh, me.c, me.y, me.xl))
+
+    @pl.when(me.mid == 0)
+    def _():
+        for z2 in range(4):
+            greet(me.device(z2, 1 - me.xh, me.c, me.y, 1 - me.xl))
+
+    for far in range(2):
+        x2 = 3 * me.xh if far else 1 + me.xl
+        for y2 in range(4):
+            for c2 in range(2):
+                device = me.device(me.z, x2 // 2, c2, y2, x2 % 2)
+                if far:
+
+                    @pl.when(jnp.logical_not(me.is_me(device)))
+                    def _():
+                        greet(device)
+
+                else:
+                    greet(device)
+
     has_low_x, has_high_x = me.w > 0, me.w < 15
     has_low_y, has_high_y = me.n > 0, me.n < 7
     low_x, high_x = (me.w - 1, me.n), (me.w + 1, me.n)
@@ -212,17 +201,9 @@
         def _():
             greet(device)
 
-    def not_me(device):
-        return 1 - me.is_me(device).astype(jnp.int32)
-
-    expected = 0
+    expected = 3 + 4 * (1 - me.mid) + 15 + me.mid
     for here, _ in sides:
         expected = expected + here.astype(jnp.int32)
-    for i in range(8):
-        expected = expected + not_me(me.first_leg(i // 2, i % 2, 0)[1])
-    for i in range(16):
-        expected = expected + not_me(me.second_leg(i // 4, (i // 2) % 2, i % 2)[1])
-        expected = expected + not_me(me.slab(i))
 
     for copy in loads[:5]:
         copy.wait()
@@ -250,42 +231,23 @@
         def _():
             remote(source, target, send, recv, device).start()
 
-    def await_send(source, send, device):
-        @pl.when(jnp.logical_not(me.is_me(device)))
-        def _():
-            remote(source, source, send, send, device).wait_send()
-
-    def await_recv(target, recv):
-        pltpu.make_async_copy(target, target, recv).wait()
-
-    def message(field, slot):
-        return sb.at[field, slot]
+    def await_bytes(ref, sem):
+        pltpu.make_async_copy(ref, ref, sem).wait()
 
     def brick_slot(field, slot):
         return rb.at[field, pl.ds(pl.multiple_of((slot + 1) * MSG, 8), MSG), :]
 
-    def route(i):
-        dz, a, c2 = i // 4, (i // 2) % 2, i % 2
-        return dz, a, c2
-
-    def leg_two(field, i, source, finish=False):
-        dz, a, c2 = route(i)
-        slot, brick, there = me.second_leg(dz, a, c2)
-        if finish:
-            await_send(source, leg2_send.at[field, slot], brick)
-        else:
-            start_any(
-                source,
-                brick_slot(field, there),
-                leg2_send.at[field, slot],
-                leg2_recv.at[field, there],
-                brick,
-            )
-
     def send_slabs(field):
         def one(i, _):
-            dz, a, c2 = route(i)
-            block, relay, slot, stays = me.first_leg(dz, a, c2)
+            send_slab(field, i)
+            return 0
+
+        lax.fori_loop(0, 8, one, 0)
+
+    def send_slab(field, i):
+        pair, relay = me.first_leg(i)
+        for c2 in range(2):
+            block = pair * 2 + c2
             x_at = block * NX - 2 + lax.broadcasted_iota(jnp.int32, (PITCH, 128), 0)
             inside = both(x_at >= 0, x_at < slab_rows // 2)
             for column in range(2):
@@ -298,46 +260,29 @@
                     else:
                         term = (vel_coeff[level] * (1.0 - t * t)) * st[level, rows, :]
                     total = term if total is None else total + term
-                sb[field, block, pl.ds(column * PITCH, PITCH), :] = jnp.where(inside, total, 0.0)
-
-            @pl.when(stays)
-            def _():
-                leg_two(field, i, message(field, block))
-
-            @pl.when(jnp.logical_not(stays))
-            def _():
-                remote(
-                    message(field, block),
-                    hb.at[field, slot],
-                    leg1_send.at[field, block],
-                    leg1_recv.at[field, slot],
-                    relay,
-                ).start()
-
-            return 0
-
-        lax.fori_loop(0, 16, one, 0)
-
-    def relay_slabs(field):
-        def one(i, _):
-            dz, a, c2 = route(i)
-            stays = me.first_leg(dz, a, c2)[3]
-            slot = me.second_leg(dz, a, c2)[0]
-
-            @pl.when(jnp.logical_not(stays))
-            def _():
-                await_recv(hb.at[field, slot], leg1_recv.at[field, slot])
-                leg_two(field, i, hb.at[field, slot])
-
-            return 0
-
-        lax.fori_loop(0, 16, one, 0)
+                sb[field, i, pl.ds((c2 * 2 + column) * PITCH, PITCH), :] = jnp.where(
+                    inside, total, 0.0
+                )
+        start_any(
+            sb.at[field, i], hb.at[field, i], leg1_send.at[field], leg1_recv.at[field, i], relay
+        )
+
+    def relay_slab(field, i):
+        await_bytes(hb.at[field, i], leg1_recv.at[field, i])
+        for c2 in range(2):
+            brick, slot = me.second_leg(i, c2)
+            which = (slot > 0).astype(jnp.int32) + (slot > 14).astype(jnp.int32)
+            start_any(
+                hb.at[field, i, pl.ds(c2 * MSG, MSG), :],
+                brick_slot(field, slot),
+                leg2_send.at[field],
+                leg2_recv.at[field, which],
+                brick,
+            )
 
     loads[5].wait()
     pl.semaphore_wait(barrier, expected)
     send_slabs(0)
-    loads[6].wait()
-    send_slabs(1)
 
     loads[7].wait()
     loads[8].wait()
@@ -387,14 +332,21 @@
 
     lax.fori_loop(2, NX - 2, inner_row, 0)
 
-    relay_slabs(0)
+    loads[6].wait()
+
+    def relay_and_send(i, _):
+        relay_slab(0, i)
+        send_slab(1, i)
+        return 0
+
+    lax.fori_loop(0, 8, relay_and_send, 0)
 
     for side in range(2):
         rows = pl.ds(0, 2 * NY * 2)
 
         @pl.when(sides[side][0])
         def _():
-            await_recv(xr.at[side], xh_recv.at[side])
+            await_bytes(xr.at[side], xh_recv.at[side])
 
         @pl.when(jnp.logical_not(sides[side][0]))
         def _():
@@ -431,7 +383,7 @@
 
             @pl.when(sides[2 + side][0])
             def _():
-                await_recv(
+                await_bytes(
                     ref.at[field, pl.ds(side * (NY + 2) * PITCH, MSG), :], recv.at[field, side]
                 )
 
@@ -445,23 +397,9 @@
     for field in range(2):
         y_halo_start(db, yd_send, yd_recv, field)
 
-    relay_slabs(1)
-
-    def arrive(field):
-        for slot in (0, 15):
-            await_recv(brick_slot(field, slot), leg2_recv.at[field, slot])
-        y_halo_start(rb, yv_send, yv_recv, field)
-
-        def one(slot, _):
-            await_recv(brick_slot(field, slot), leg2_recv.at[field, slot])
-            return 0
-
-        lax.fori_loop(1, 15, one, 0)
-
-    arrive(0)
-    for field in range(2):
-        y_halo_recv(db, yd_send, yd_recv, field)
-    y_halo_recv(rb, yv_send, yv_recv, 0)
+    def relay_second(i, _):
+        relay_slab(1, i)
+        return 0
 
     def gradient(ref, field, yy):
         def at(column, x):
@@ -473,65 +411,145 @@
             depth_change(at(yy, 0)),
         )
 
-    def edge_gradient(ref, field, x):
+    def edge_gradient(ref, field, side, rows):
+        x = (-1, NX)[side]
+
         def at(dy, x):
-            return ref[field, pl.ds((2 + dy) * PITCH + 2 + x, NY, stride=PITCH), :]
+            start = (rows.start + 2 + dy) * PITCH + 2 + x
+            return ref[field, pl.ds(start, rows.size, stride=PITCH), :]
 
         return (at(0, x + 1) - at(0, x - 1), at(1, x) - at(-1, x), depth_change(at(0, x)))
 
+    every, inner_rows = pl.ds(0, NY), pl.ds(1, NY - 2)
+
+    def keep(ref, *at_and_vector):
+        *at, vector = at_and_vector
+        for number in range(3):
+            ref[(at[0], number, *at[1:])] = vector[number]
+
+    def kept(ref, *at):
+        return tuple(ref[(at[0], number, *at[1:])] for number in range(3))
+
+    def columns(body, first, count, batch):
+        def some(j, _):
+            body([first + j * batch + k for k in range(batch)])
+            return 0
+
+        lax.fori_loop(0, count // batch, some, 0)
+
+    def dens_gradient(field):
+        def some(yys):
+            for yy in yys:
+                keep(grads, field, yy, gradient(db, field, yy))
+
+        columns(some, 2, NY, 4)
+        some([1, NY + 2])
+        for side in range(2):
+            keep(edge_grads, field, side, every, edge_gradient(db, field, side, every))
+
+    def mixed(field, own, grads, *at):
+        first = cross(kept(grads, 0, *at), own)
+        if field == 0:
+            return first
+        second = cross(kept(grads, 1, *at), kept(grads, 2, *at))
+        return tuple(s + t for s, t in zip(second, first))
+
+    def masked(vector, inside):
+        factor = inside.astype(jnp.float32)
+        return tuple(v * factor for v in vector)
+
+    def vel_columns(field, yys, inside=None):
+        qs = []
+        for number, yy in enumerate(yys):
+            own = gradient(rb, field, yy)
+            mix = mixed(field, own, grads, yy)
+            if inside is not None:
+                mix = masked(mix, inside[number])
+            keep(grads, 2 + field, yy, own)
+            keep(mixes, field, yy, mix)
+            qs.append(cross(mix, kept(grads, 0, yy)))
+        collect(qs, yys)
+
+    def vel_edges(field, rows):
+        for side in range(2):
+            own = edge_gradient(rb, field, side, rows)
+            mix = masked(mixed(field, own, edge_grads, side, rows), sides[side][0])
+            keep(edge_grads, 2 + field, side, rows, own)
+            keep(edge_mixes, field, side, rows, mix)
+            dens = kept(edge_grads, 0, side, rows)
+            q1e[side, rows] = mix[1] * dens[2] - mix[2] * dens[1]
+
+    def dens_columns(field, yys):
+        collect([cross(kept(grads, 2, yy), kept(mixes, field, yy)) for yy in yys], yys)
+
+    def dens_edges(field):
+        for side in range(2):
+            vel, mix = kept(edge_grads, 2, side, every), kept(edge_mixes, field, side, every)
+            q1e[side] = vel[1] * mix[2] - vel[2] * mix[1]
+
+    def collect(qs, yys):
+        for k, (q, yy) in enumerate(zip(qs, yys)):
+            y = jnp.clip(yy - 2, 0, NY - 1)
+            q1s[k, pl.ds(8, NX), :] = q[0]
+            q1s[k, pl.ds(7, 1), :] = q1e[0, pl.ds(y, 1), :]
+            q1s[k, pl.ds(8 + NX, 1), :] = q1e[1, pl.ds(y, 1), :]
+            q2s[yy] = q[1]
+        turned = [depth_change(q[2]) for q in qs]
+        for k, yy in enumerate(yys):
+            acc[yy] = q1s[k, pl.ds(7, NX), :] - q1s[k, pl.ds(9, NX), :] - turned[k]
+
+    def adjoint(yy):
+        return acc[yy] + (q2s[yy - 1] - q2s[yy + 1])
+
     def compute(field):
-        which = [(db, 0), (rb, 0), (db, 1), (rb, 1)][: 2 + 2 * field]
-
-        for side in range(2):
-            x = (-1, NX)[side]
-            dens, vel, mixed = coupled(field, [edge_gradient(r, f, x) for r, f in which])
-            keep = sides[side][0].astype(jnp.float32)
-            q1e[0, side] = cross_first(vel, mixed) * keep
-            q1e[1, side] = cross_first(mixed, dens) * keep
-
-        def column(yy):
-            dens, vel, mixed = coupled(field, [gradient(r, f, yy) for r, f in which])
-            outside = jnp.logical_or(
-                both(yy == 1, me.n == 0), both(yy == NY + 2, me.n == 7)
-            )
-            keep = 1.0 - outside.astype(jnp.float32)
-            y = jnp.clip(yy - 2, 0, NY - 1)
-            for out, q in enumerate((cross(vel, mixed), cross(mixed, dens))):
-                q1s[out, pl.ds(8, NX), :] = q[0]
-                q1s[out, pl.ds(7, 1), :] = q1e[out, 0, pl.ds(y, 1), :]
-                q1s[out, pl.ds(8 + NX, 1), :] = q1e[out, 1, pl.ds(y, 1), :]
-                along_x = q1s[out, pl.ds(7, NX), :] - q1s[out, pl.ds(9, NX), :]
-                q2s[out, yy] = q[1] * keep
-                acc[out, yy] = along_x - depth_change(q[2])
-
-        column(1)
-        column(2)
-
-        def pair(p, _):
-            for half in range(2):
-                yy = 2 * p + 2 + half
-                column(yy + 1)
-                df[field, pl.ds(pl.multiple_of((yy - 2) * NX, 8), NX), :] = acc[0, yy] + (
-                    q2s[0, yy - 1] - q2s[0, yy + 1]
+        vel_edges(field, inner_rows)
+
+        columns(lambda yys: vel_columns(field, yys), 3, NY - 2, 5)
+        y_halo_recv(rb, yv_send, yv_recv, field)
+        vel_edges(field, every)
+        true = me.n >= 0
+        vel_columns(field, [1, 2, NY + 1, NY + 2], [me.n > 0, true, true, me.n < 7])
+
+        def back(i, _):
+            for c2 in range(2):
+                p, slab = me.way_back(i, c2)
+                for half in range(2):
+                    rs[field, p, pl.ds(half * NX, NX), :] = adjoint(2 * p + 2 + half)
+                start_any(
+                    rs.at[field, p], rv.at[field, me.w], ret_send.at[field], ret_recv.at[field], slab
                 )
-                rs[field, p, pl.ds(half * NX, NX), :] = acc[1, yy] + (
-                    q2s[1, yy - 1] - q2s[1, yy + 1]
-                )
-            start_any(
-                rs.at[field, p],
-                rv.at[field, me.w],
-                ret_send.at[field, p],
-                ret_recv.at[field, me.w],
-                me.slab(p),
-            )
             return 0
 
-        lax.fori_loop(0, 16, pair, 0)
-
+        lax.fori_loop(0, 8, back, 0)
+
+    def arrive(field):
+        for slot in (0, 15):
+            await_bytes(brick_slot(field, slot), leg2_recv.at[field, slot // 15 * 2])
+        y_halo_start(rb, yv_send, yv_recv, field)
+        await_bytes(rb.at[field, pl.ds(2 * MSG, 14 * MSG), :], leg2_recv.at[field, 1])
+
+    for field in range(2):
+        y_halo_recv(db, yd_send, yd_recv, field)
+        dens_gradient(field)
+    lax.fori_loop(0, 8, relay_second, 0)
+    arrive(0)
     compute(0)
     arrive(1)
-    y_halo_recv(rb, yv_send, yv_recv, 1)
     compute(1)
+
+    for field in range(2):
+        dens_edges(field)
+
+        columns(lambda yys: dens_columns(field, yys), 2, NY, 4)
+        dens_columns(field, [1, NY + 2])
+
+        def keep_force(y, _):
+            for k in range(4):
+                at = pl.ds(pl.multiple_of((4 * y + k) * NX, 8), NX)
+                df[field, at, :] = adjoint(4 * y + k + 2)
+            return 0
+
+        lax.fori_loop(0, NY // 4, keep_force, 0)
 
     for field in range(2):
 
@@ -552,8 +570,9 @@
 
     for field in range(2):
 
+        await_bytes(rv.at[field], ret_recv.at[field])
+
         def finish(block, _):
-            await_recv(rv.at[field, block], ret_recv.at[field, block])
             for half in range(2):
                 vel_out[field, pl.ds(block * 2 * NX + half, NX, stride=2), :] = rv[
                     field, block, pl.ds(half * NX, NX), :
@@ -572,25 +591,21 @@
         y_halo_sent(db, yd_send, yd_recv, field)
         y_halo_sent(rb, yv_send, yv_recv, field)
 
-        def sent(i, _):
-            dz, a, c2 = route(i)
-            block, relay, slot, stays = me.first_leg(dz, a, c2)
-
-            @pl.when(jnp.logical_not(stays))
-            def _():
-                remote(
-                    message(field, block),
-                    message(field, block),
-                    leg1_send.at[field, block],
-                    leg1_send.at[field, block],
-                    relay,
-                ).wait_send()
-
-            leg_two(field, i, hb.at[field, 0], finish=True)
-            await_send(rs.at[field, 0], ret_send.at[field, i], me.slab(i))
-            return 0
-
-        lax.fori_loop(0, 16, sent, 0)
+        await_bytes(sb.at[field, pl.ds(0, 6)], leg1_send.at[field])
+        await_bytes(rb.at[field, pl.ds(0, 15 * MSG), :], leg2_send.at[field])
+        await_bytes(rs.at[field, pl.ds(0, 15)], ret_send.at[field])
+
+        @pl.when(me.mid == 0)
+        def _():
+            await_bytes(sb.at[field, 0], leg1_send.at[field])
+
+        @pl.when(me.mid == 1)
+        def _():
+            await_bytes(rb.at[field, pl.ds(0, MSG), :], leg2_send.at[field])
+
+        @pl.when(me.w // 2 != me.n)
+        def _():
+            await_bytes(rs.at[field, 0], ret_send.at[field])
 
 
 def chain_kernel(
@@ -655,35 +670,39 @@
             pltpu.VMEM((levels, nx, ny, nz), f32),
             pltpu.VMEM((levels, rows + 4 * PAD, nz), f32),
             pltpu.VMEM((levels, rows + 4 * PAD, nz), f32),
-            pltpu.VMEM((2, 16, MSG, nz), f32),
-            pltpu.VMEM((2, 16, MSG, nz), f32),
+            pltpu.VMEM((2, 8, 2 * MSG, nz), f32),
+            pltpu.VMEM((2, 8, 2 * MSG, nz), f32),
             pltpu.VMEM((2, COLS, nz), f32),
             pltpu.VMEM((2, COLS, nz), f32),
             pltpu.VMEM((2, 4 * NY, nz), f32),
             pltpu.VMEM((2, 4 * NY, nz), f32),
-            pltpu.VMEM((2, 2, NY, nz), f32),
-            pltpu.VMEM((2, NX + 16, nz), f32),
-            pltpu.VMEM((2, NY + 4, NX, nz), f32),
-            pltpu.VMEM((2, NY + 4, NX, nz), f32),
+            pltpu.VMEM((4, 3, NY + 4, NX, nz), f32),
+            pltpu.VMEM((4, 3, 2, NY, nz), f32),
+            pltpu.VMEM((2, 3, NY + 4, NX, nz), f32),
+            pltpu.VMEM((2, 3, 2, NY, nz), f32),
+            pltpu.VMEM((2, NY, nz), f32),
+            pltpu.VMEM((5, NX + 16, nz), f32),
+            pltpu.VMEM((NY + 4, NX, nz), f32),
+            pltpu.VMEM((NY + 4, NX, nz), f32),
             pltpu.VMEM((2, NY * NX, nz), f32),
             pltpu.VMEM((2, 16, 2 * NX, nz), f32),
             pltpu.VMEM((2, 16, 2 * NX, nz), f32),
             dma((9,)),
-            dma((2, 16)),
-            dma((2, 16)),
-            dma((2, 16)),
-            dma((2, 16)),
+            dma((2,)),
+            dma((2, 8)),
+            dma((2,)),
+            dma((2, 3)),
             dma((2,)),
             dma((2,)),
             dma((2, 2)),
             dma((2, 2)),
             dma((2, 2)),
             dma((2, 2)),
-            dma((2, 16)),
-            dma((2, 16)),
+            dma((2,)),
+            dma((2,)),
         ],
         compiler_params=pltpu.CompilerParams(
-            collective_id=0, has_side_effects=True, vmem_limit_bytes=40 << 20
+            collective_id=0, has_side_effects=True, vmem_limit_bytes=42 << 20
         ),
         name="forces",
     )(*(pltpu.with_memory_space_constraint(v, pltpu.HBM) for v in (grav_levels, grav_step, seis_rows, step_rows, *tables)))

time: 63.2 us -> 57.1 us (0.903)
  Pallas kernels: 61.9 us -> 55.7 us
    pallas_call x1, Pallas kernels: 57.4 us -> 51.3 us  [shards(): pl.pallas_call(forces_kernel, out_shape=(jax.ShapeDtypeStruct((2, nx, ny,...]
where the time goes in v3:
time: 57.1 us; the launch traced here: 56.4 us
  Pallas kernels  55.7 us (98%)
  between operations  0.64 us (1%)
    pallas_call x1, Pallas kernels, shards(): pl.pallas_call(forces_kernel, out_shape=(jax.ShapeDtypeStruct((2, nx, ny,...  51.3 us
    pallas_call x1, Pallas kernels, shards(): pl.pallas_call(functools.partial(chain_kernel, steps), grid=(steps,), out...  4.46 us

profile of v3, /device:TPU:65, one launch (start us, length us, event | category | flops | bytes accessed | tf_op | source)
XLA Modules:
  0.0 56.4 jit_solution(10287668348247015119)
XLA Ops:
  0.6 51.3 %forces.1 = (f32[2,32,32,128]{3,2,1,0:T(8,128)S(1)}, f32[2,1024,128]{2,1,0:T(8,128)S(1)}, f32[4,32,32,128]{3,2,1,0:T(8,128)S(1)}, f32[4,1024,128]{2,1,0:T(8,128)S(1)}) custom-call(f32[4,32,32,128]{3,2,1,0:T(8,128)} %grav_levels.1, f32[4,32,32,128]{3,2,1,0:T(8,128)} %grav_step.1, f32[4,1024,128]{2,1,0:T(8,128)} %bitcast.4, f32[4,1024,128]{2,1,0:T(8,128)} %bitcast.5, ...), custom_call_target="tpu_custom_call" | custom-call | tf_op jit(solution)/shard_map/forces/pallas_call | solution.py:657
  51.9 4.5 %chain.1 = (f32[4,32,32,128]{3,2,1,0:T(8,128)}, f32[4,32,32,128]{3,2,1,0:T(8,128)}, f32[4,1024,128]{2,1,0:T(8,128)}, f32[4,1024,128]{2,1,0:T(8,128)}) custom-call(f32[2,32,32,128]{3,2,1,0:T(8,128)S(1)} %get-tuple-element.12.dens_force, f32[2,1024,128]{2,1,0:T(8,128)S(1)} %get-tuple-element.13.vel_force, f32[4,32,32,128]{3,2,1,0:T(8,128)S(1)} %get-tuple-element.14.grav_slope, ...), custom_call_target="tpu_custom_call" | custom-call | tf_op jit(solution)/shard_map/chain/pallas_call | solution.py:713

commit v4 on v3

--- a/solution.py
+++ b/solution.py
@@ -117,6 +117,10 @@
     db,
     xs,
     xr,
+    ys,
+    yr,
+    cs,
+    cr,
     grads,
     edge_grads,
     mixes,
@@ -137,6 +141,8 @@
     xh_recv,
     yd_send,
     yd_recv,
+    co_send,
+    co_recv,
     yv_send,
     yv_recv,
     ret_send,
@@ -195,14 +201,19 @@
     low_x, high_x = (me.w - 1, me.n), (me.w + 1, me.n)
     low_y, high_y = (me.w, me.n - 1), (me.w, me.n + 1)
     sides = ((has_low_x, low_x), (has_high_x, high_x), (has_low_y, low_y), (has_high_y, high_y))
-    for here, device in sides:
+    corners = [
+        (both(sides[sx][0], sides[2 + sy][0]), (me.w + 2 * sx - 1, me.n + 2 * sy - 1))
+        for sx in range(2)
+        for sy in range(2)
+    ]
+    for here, device in (*sides, *corners):
 
         @pl.when(here)
         def _():
             greet(device)
 
     expected = 3 + 4 * (1 - me.mid) + 15 + me.mid
-    for here, _ in sides:
+    for here, _ in (*sides, *corners):
         expected = expected + here.astype(jnp.int32)
 
     for copy in loads[:5]:
@@ -332,6 +343,37 @@
 
     lax.fori_loop(2, NX - 2, inner_row, 0)
 
+    for side in range(2):
+        for field in range(2):
+            for column in range(2):
+                ys[side, pl.ds((field * 2 + column) * NX, NX), :] = db[
+                    field, pl.ds((2 + side * (NY - 2) + column) * PITCH + 2, NX), :
+                ]
+    cs[...] = jnp.zeros(cs.shape, jnp.float32)
+    for k in range(4):
+        at = (2 + k % 2 * (NY - 1)) * PITCH + 2 + k // 2 * (NX - 1)
+        for field in range(2):
+            cs[k, pl.ds(field, 1), :] = db[field, pl.ds(at, 1), :]
+
+    def y_side(side):
+        return remote(
+            ys.at[side], yr.at[1 - side], yd_send.at[side], yd_recv.at[1 - side], sides[2 + side][1]
+        )
+
+    def corner(k):
+        return remote(cs.at[k], cr.at[3 - k], co_send.at[k], co_recv.at[3 - k], corners[k][1])
+
+    dens_halos = [
+        *((sides[side][0], x_halo(side), xr.at[side], xh_recv.at[side]) for side in range(2)),
+        *((sides[2 + side][0], y_side(side), yr.at[side], yd_recv.at[side]) for side in range(2)),
+        *((corners[k][0], corner(k), cr.at[k], co_recv.at[k]) for k in range(4)),
+    ]
+    for here, copy, _, _ in dens_halos[2:]:
+
+        @pl.when(here)
+        def _():
+            copy.start()
+
     loads[6].wait()
 
     def relay_and_send(i, _):
@@ -341,65 +383,76 @@
 
     lax.fori_loop(0, 8, relay_and_send, 0)
 
-    for side in range(2):
-        rows = pl.ds(0, 2 * NY * 2)
-
-        @pl.when(sides[side][0])
-        def _():
-            await_bytes(xr.at[side], xh_recv.at[side])
-
-        @pl.when(jnp.logical_not(sides[side][0]))
-        def _():
-            xr[side] = jnp.zeros(xr.shape[1:], jnp.float32)
-
-        for field in range(2):
+    def y_halo(field, side):
+        source = rb.at[field, pl.ds((2 + side * (NY - 2)) * PITCH, MSG), :]
+        target = rb.at[field, pl.ds((1 - side) * (NY + 2) * PITCH, MSG), :]
+        return remote(
+            source, target, yv_send.at[field, side], yv_recv.at[field, 1 - side], (low_y, high_y)[side]
+        )
+
+    def y_halo_start(field):
+        for side in range(2):
+
+            @pl.when(sides[2 + side][0])
+            def _():
+                y_halo(field, side).start()
+
+            @pl.when(jnp.logical_not(sides[2 + side][0]))
+            def _():
+                rb[field, pl.ds(side * (NY + 2) * PITCH, MSG), :] = jnp.zeros(
+                    (MSG, 128), jnp.float32
+                )
+
+    def y_halo_recv(field):
+        for side in range(2):
+
+            @pl.when(sides[2 + side][0])
+            def _():
+                await_bytes(
+                    rb.at[field, pl.ds(side * (NY + 2) * PITCH, MSG), :], yv_recv.at[field, side]
+                )
+
+    def y_halo_sent(field):
+        for side in range(2):
+
+            @pl.when(sides[2 + side][0])
+            def _():
+                y_halo(field, side).wait_send()
+
+    def y_halo_early(field):
+        for slot in (0, 15):
+            await_bytes(brick_slot(field, slot), leg2_recv.at[field, slot // 15 * 2])
+        y_halo_start(field)
+
+    def relay_second(i, _):
+        relay_slab(1, i)
+        return 0
+
+    lax.fori_loop(0, 8, relay_second, 0)
+    y_halo_early(0)
+
+    for here, _, ref, recv in dens_halos:
+
+        @pl.when(here)
+        def _():
+            await_bytes(ref, recv)
+
+        @pl.when(jnp.logical_not(here))
+        def _():
+            ref[...] = jnp.zeros(ref.shape, jnp.float32)
+
+    for field in range(2):
+        for side in range(2):
             for row in range(2):
                 db[field, pl.ds(2 * PITCH + side * (NX + 2) + row, NY, stride=PITCH), :] = xr[
                     side, pl.ds((field * 2 + row) * NY, NY), :
                 ]
-
-    def y_halo(ref, send, recv, field, side):
-        source = ref.at[field, pl.ds((2 + side * (NY - 2)) * PITCH, MSG), :]
-        target = ref.at[field, pl.ds((1 - side) * (NY + 2) * PITCH, MSG), :]
-        return remote(
-            source, target, send.at[field, side], recv.at[field, 1 - side], (low_y, high_y)[side]
-        )
-
-    def y_halo_start(ref, send, recv, field):
-        for side in range(2):
-
-            @pl.when(sides[2 + side][0])
-            def _():
-                y_halo(ref, send, recv, field, side).start()
-
-            @pl.when(jnp.logical_not(sides[2 + side][0]))
-            def _():
-                ref[field, pl.ds(side * (NY + 2) * PITCH, MSG), :] = jnp.zeros(
-                    (MSG, 128), jnp.float32
-                )
-
-    def y_halo_recv(ref, send, recv, field):
-        for side in range(2):
-
-            @pl.when(sides[2 + side][0])
-            def _():
-                await_bytes(
-                    ref.at[field, pl.ds(side * (NY + 2) * PITCH, MSG), :], recv.at[field, side]
-                )
-
-    def y_halo_sent(ref, send, recv, field):
-        for side in range(2):
-
-            @pl.when(sides[2 + side][0])
-            def _():
-                y_halo(ref, send, recv, field, side).wait_send()
-
-    for field in range(2):
-        y_halo_start(db, yd_send, yd_recv, field)
-
-    def relay_second(i, _):
-        relay_slab(1, i)
-        return 0
+                db[field, pl.ds((side * (NY + 2) + row) * PITCH + 2, NX), :] = yr[
+                    side, pl.ds((field * 2 + row) * NX, NX), :
+                ]
+        for k in range(4):
+            at = (1 + k % 2 * (NY + 1)) * PITCH + 1 + k // 2 * (NX + 1)
+            db[field, pl.ds(at, 1), :] = cr[k, pl.ds(field, 1), :]
 
     def gradient(ref, field, yy):
         def at(column, x):
@@ -505,7 +558,9 @@
         vel_edges(field, inner_rows)
 
         columns(lambda yys: vel_columns(field, yys), 3, NY - 2, 5)
-        y_halo_recv(rb, yv_send, yv_recv, field)
+        if field == 0:
+            y_halo_early(1)
+        y_halo_recv(field)
         vel_edges(field, every)
         true = me.n >= 0
         vel_columns(field, [1, 2, NY + 1, NY + 2], [me.n > 0, true, true, me.n < 7])
@@ -523,15 +578,10 @@
         lax.fori_loop(0, 8, back, 0)
 
     def arrive(field):
-        for slot in (0, 15):
-            await_bytes(brick_slot(field, slot), leg2_recv.at[field, slot // 15 * 2])
-        y_halo_start(rb, yv_send, yv_recv, field)
         await_bytes(rb.at[field, pl.ds(2 * MSG, 14 * MSG), :], leg2_recv.at[field, 1])
 
     for field in range(2):
-        y_halo_recv(db, yd_send, yd_recv, field)
         dens_gradient(field)
-    lax.fori_loop(0, 8, relay_second, 0)
     arrive(0)
     compute(0)
     arrive(1)
@@ -581,15 +631,14 @@
 
         lax.fori_loop(0, 16, finish, 0)
 
-    for side in range(2):
-
-        @pl.when(sides[side][0])
-        def _():
-            x_halo(side).wait_send()
+    for here, copy, _, _ in dens_halos:
+
+        @pl.when(here)
+        def _():
+            copy.wait_send()
 
     for field in range(2):
-        y_halo_sent(db, yd_send, yd_recv, field)
-        y_halo_sent(rb, yv_send, yv_recv, field)
+        y_halo_sent(field)
 
         await_bytes(sb.at[field, pl.ds(0, 6)], leg1_send.at[field])
         await_bytes(rb.at[field, pl.ds(0, 15 * MSG), :], leg2_send.at[field])
@@ -676,6 +725,10 @@
             pltpu.VMEM((2, COLS, nz), f32),
             pltpu.VMEM((2, 4 * NY, nz), f32),
             pltpu.VMEM((2, 4 * NY, nz), f32),
+            pltpu.VMEM((2, 4 * NX, nz), f32),
+            pltpu.VMEM((2, 4 * NX, nz), f32),
+            pltpu.VMEM((4, 8, nz), f32),
+            pltpu.VMEM((4, 8, nz), f32),
             pltpu.VMEM((4, 3, NY + 4, NX, nz), f32),
             pltpu.VMEM((4, 3, 2, NY, nz), f32),
             pltpu.VMEM((2, 3, NY + 4, NX, nz), f32),
@@ -694,8 +747,10 @@
             dma((2, 3)),
             dma((2,)),
             dma((2,)),
-            dma((2, 2)),
-            dma((2, 2)),
+            dma((2,)),
+            dma((2,)),
+            dma((4,)),
+            dma((4,)),
             dma((2, 2)),
             dma((2, 2)),
             dma((2,)),

time: 57.1 us -> 51.6 us (0.904); the launches traced: 56.4 us -> 51.5 us
  Pallas kernels: 55.7 us -> 50.9 us
    pallas_call x1, Pallas kernels: 51.3 us -> 46.4 us  [shards(): pl.pallas_call(forces_kernel, out_shape=(jax.ShapeDtypeStruct((2, nx, ny,...]
where the time goes in v4:
time: 51.6 us; the launch traced here: 51.5 us
  Pallas kernels  50.9 us (99%)
  between operations  0.64 us (1%)
    pallas_call x1, Pallas kernels, shards(): pl.pallas_call(forces_kernel, out_shape=(jax.ShapeDtypeStruct((2, nx, ny,...  46.4 us
    pallas_call x1, Pallas kernels, shards(): pl.pallas_call(functools.partial(chain_kernel, steps), grid=(steps,), out...  4.46 us

profile of v4, /device:TPU:65, one launch (start us, length us, event | category | flops | bytes accessed | tf_op | source)
XLA Modules:
  0.0 51.5 jit_solution(5200218711448532538)
XLA Ops:
  0.6 46.4 %forces.1 = (f32[2,32,32,128]{3,2,1,0:T(8,128)S(1)}, f32[2,1024,128]{2,1,0:T(8,128)S(1)}, f32[4,32,32,128]{3,2,1,0:T(8,128)S(1)}, f32[4,1024,128]{2,1,0:T(8,128)S(1)}) custom-call(f32[4,32,32,128]{3,2,1,0:T(8,128)} %grav_levels.1, f32[4,32,32,128]{3,2,1,0:T(8,128)} %grav_step.1, f32[4,1024,128]{2,1,0:T(8,128)} %bitcast.4, f32[4,1024,128]{2,1,0:T(8,128)} %bitcast.5, ...), custom_call_target="tpu_custom_call" | custom-call | tf_op jit(solution)/shard_map/forces/pallas_call | solution.py:706
  47.1 4.5 %chain.1 = (f32[4,32,32,128]{3,2,1,0:T(8,128)}, f32[4,32,32,128]{3,2,1,0:T(8,128)}, f32[4,1024,128]{2,1,0:T(8,128)}, f32[4,1024,128]{2,1,0:T(8,128)}) custom-call(f32[2,32,32,128]{3,2,1,0:T(8,128)S(1)} %get-tuple-element.12.dens_force, f32[2,1024,128]{2,1,0:T(8,128)S(1)} %get-tuple-element.13.vel_force, f32[4,32,32,128]{3,2,1,0:T(8,128)S(1)} %get-tuple-element.14.grav_slope, ...), custom_call_target="tpu_custom_call" | custom-call | tf_op jit(solution)/shard_map/chain/pallas_call | solution.py:768

commit v5 on v4

--- a/solution.py
+++ b/solution.py
@@ -154,12 +154,12 @@
     loads = []
     for number, (source, target) in enumerate(
         [
+            (seis_levels, sl.at[:, pl.ds(PAD, slab_rows), :]),
             (labels_in, labels),
             (dens_index_in, dens_index),
             (vel_index_in, vel_index),
             (dens_table_in, dens_table),
             (vel_table_in, vel_table),
-            (seis_levels, sl.at[:, pl.ds(PAD, slab_rows), :]),
             (seis_step, st.at[:, pl.ds(PAD, slab_rows), :]),
             (grav_levels, gl),
             (grav_step, gs),
@@ -216,7 +216,7 @@
     for here, _ in (*sides, *corners):
         expected = expected + here.astype(jnp.int32)
 
-    for copy in loads[:5]:
+    for copy in loads[1:6]:
         copy.wait()
     dens_coeff = [0.5 * v for v in coeffs(labels, dens_index, dens_table)]
     vel_coeff = [0.5 * v for v in coeffs(labels, vel_index, vel_table)]
@@ -291,7 +291,7 @@
                 brick,
             )
 
-    loads[5].wait()
+    loads[0].wait()
     pl.semaphore_wait(barrier, expected)
     send_slabs(0)
 
@@ -667,17 +667,33 @@
     grav_curvature,
     seis_gradient,
     seis_curvature,
+    brick_outs,
+    slab_outs,
+    sems,
 ):
-    for slope, force, outs in (
-        (grav_slope, dens_force, (grav_gradient, grav_curvature)),
-        (seis_slope, vel_force, (seis_gradient, seis_curvature)),
-    ):
-        rows = slope.shape[1] // steps
-        here = pl.ds(pl.program_id(0) * rows, rows)
-        for level in range(4):
-            factor = slope[level, here]
+    parts = (
+        (grav_slope, dens_force, (grav_gradient, grav_curvature), brick_outs, 0),
+        (seis_slope, vel_force, (seis_gradient, seis_curvature), slab_outs, 2),
+    )
+
+    def step(i, _):
+        for slope, force, outs, made, sem in parts:
+            rows = slope.shape[1] // steps
+            here = pl.ds(i * rows, rows)
+            for level in range(4):
+                factor = slope[level, here]
+                for number in range(2):
+                    made[number, level, here] = factor * force[number, here]
             for number in range(2):
-                outs[number][level] = factor * force[number, here]
+                pltpu.make_async_copy(
+                    made.at[number, :, here], outs[number].at[:, here], sems.at[sem + number]
+                ).start()
+        return 0
+
+    lax.fori_loop(0, steps, step, 0)
+    for _, _, outs, made, sem in parts:
+        for number in range(2):
+            pltpu.make_async_copy(made.at[number], outs[number], sems.at[sem + number]).wait()
 
 
 def shards(
@@ -762,15 +778,16 @@
         name="forces",
     )(*(pltpu.with_memory_space_constraint(v, pltpu.HBM) for v in (grav_levels, grav_step, seis_rows, step_rows, *tables)))
 
-    steps = 8
-    brick = pl.BlockSpec((levels, nx // steps, ny, nz), lambda i: (0, i, 0, 0))
-    slab = pl.BlockSpec((levels, rows // steps, nz), lambda i: (0, i, 0))
     outs = pl.pallas_call(
-        functools.partial(chain_kernel, steps),
-        grid=(steps,),
+        functools.partial(chain_kernel, 8),
         out_shape=(brick_shape, brick_shape, slab_shape, slab_shape),
         in_specs=[vmem] * 4,
-        out_specs=(brick, brick, slab, slab),
+        out_specs=(hbm,) * 4,
+        scratch_shapes=[
+            pltpu.VMEM((2, *brick_shape.shape), f32),
+            pltpu.VMEM((2, *slab_shape.shape), f32),
+            dma((4,)),
+        ],
         compiler_params=pltpu.CompilerParams(vmem_limit_bytes=32 << 20),
         name="chain",
     )(*forces)

time: 51.6 us -> 50.5 us (0.979)
  Pallas kernels: 50.9 us -> 49.8 us
    pallas_call x1, Pallas kernels: 4.46 us -> 3.33 us  [shards(): pl.pallas_call(functools.partial(chain_kernel, 8), out_shape=(brick_shape...]
where the time goes in v5:
time: 50.5 us; the launch traced here: 50.4 us
  Pallas kernels  49.8 us (99%)
  between operations  0.64 us (1%)
    pallas_call x1, Pallas kernels, shards(): pl.pallas_call(forces_kernel, out_shape=(jax.ShapeDtypeStruct((2, nx, ny,...  46.4 us
    pallas_call x1, Pallas kernels, shards(): pl.pallas_call(functools.partial(chain_kernel, 8), out_shape=(brick_shape...  3.33 us

profile of v5, /device:TPU:65, one launch (start us, length us, event | category | flops | bytes accessed | tf_op | source)
XLA Modules:
  0.0 50.4 jit_solution(15195244757390384910)
XLA Ops:
  0.6 46.4 %forces.1 = (f32[2,32,32,128]{3,2,1,0:T(8,128)S(1)}, f32[2,1024,128]{2,1,0:T(8,128)S(1)}, f32[4,32,32,128]{3,2,1,0:T(8,128)S(1)}, f32[4,1024,128]{2,1,0:T(8,128)S(1)}) custom-call(f32[4,32,32,128]{3,2,1,0:T(8,128)} %grav_levels.1, f32[4,32,32,128]{3,2,1,0:T(8,128)} %grav_step.1, f32[4,1024,128]{2,1,0:T(8,128)} %bitcast.4, f32[4,1024,128]{2,1,0:T(8,128)} %bitcast.5, ...), custom_call_target="tpu_custom_call" | custom-call | tf_op jit(solution)/shard_map/forces/pallas_call | solution.py:722
  47.1 3.3 %chain.1 = (f32[4,32,32,128]{3,2,1,0:T(8,128)}, f32[4,32,32,128]{3,2,1,0:T(8,128)}, f32[4,1024,128]{2,1,0:T(8,128)}, f32[4,1024,128]{2,1,0:T(8,128)}) custom-call(f32[2,32,32,128]{3,2,1,0:T(8,128)S(1)} %get-tuple-element.12.dens_force, f32[2,1024,128]{2,1,0:T(8,128)S(1)} %get-tuple-element.13.vel_force, f32[4,32,32,128]{3,2,1,0:T(8,128)S(1)} %get-tuple-element.14.grav_slope, ...), custom_call_target="tpu_custom_call" | custom-call | tf_op jit(solution)/shard_map/chain/pallas_call | solution.py:781

commit v6 on v5

--- a/solution.py
+++ b/solution.py
@@ -16,6 +16,14 @@
 PAD = 8
 
 
+def quotient(value, by):
+    return value // by if isinstance(value, int) else lax.div(value, jnp.int32(by))
+
+
+def rest(value, by):
+    return value % by if isinstance(value, int) else lax.rem(value, jnp.int32(by))
+
+
 def both(one, other):
     return jnp.logical_and(one, other)
 
@@ -24,13 +32,13 @@
     def __init__(self):
         self.w = lax.axis_index("wide")
         self.n = lax.axis_index("narrow")
-        self.z = self.w // 4
-        self.xh = (self.w // 2) % 2
-        self.c = self.w % 2
-        self.y = self.n // 2
-        self.xl = self.n % 2
+        self.z = quotient(self.w, 4)
+        self.xh = rest(quotient(self.w, 2), 2)
+        self.c = rest(self.w, 2)
+        self.y = quotient(self.n, 2)
+        self.xl = rest(self.n, 2)
         self.x = self.xh * 2 + self.xl
-        self.mid = (self.xh + self.xl) % 2
+        self.mid = rest(self.xh + self.xl, 2)
 
     @staticmethod
     def device(z, xh, c, y, xl):
@@ -43,8 +51,8 @@
         return self.x + (1 - self.mid) * a * (3 - 2 * self.x)
 
     def step(self, i):
-        pair, half = i // 2, i % 2
-        return pair // 2 + 2 * half, (pair + half) % 2
+        pair, half = quotient(i, 2), rest(i, 2)
+        return quotient(pair, 2) + 2 * half, rest(pair + half, 2)
 
     def side(self, e):
         return 1 - e + (1 - self.xh) * self.xl * (2 * e - 1)
@@ -52,25 +60,19 @@
     def first_leg(self, i):
         d, e = self.step(i)
         a = self.side(e)
-        z2 = (self.z + self.y + d) % 4
+        z2 = rest(self.z + self.y + d, 4)
         xr = self.across(a)
-        xh2 = self.mid * a + (1 - self.mid) * (xr // 2)
-        return z2 * 2 + xh2, self.device(z2, xr // 2, self.c, self.y, xr % 2)
+        xh2 = self.mid * a + (1 - self.mid) * quotient(xr, 2)
+        return z2 * 2 + xh2, self.device(z2, quotient(xr, 2), self.c, self.y, rest(xr, 2))
 
     def second_leg(self, i, c2):
         d, e = self.step(i)
         a = self.side(e)
-        zs = (self.z + 8 - self.y - d) % 4
+        zs = rest(self.z + 8 - self.y - d, 4)
         xs = self.across(a)
         xh2 = self.mid * a + (1 - self.mid) * self.xh
-        brick = self.device(self.z, xh2, c2, zs, xs // 2)
-        return brick, self.c * 8 + self.y * 2 + xs % 2
-
-    def way_back(self, i, c2):
-        d, e = self.step(i)
-        y2 = (self.y + self.z + d) % 4
-        pair = c2 * 8 + y2 * 2 + (self.xh + e) % 2
-        return pair, (self.n * 2 + c2, pair % 8)
+        brick = self.device(self.z, xh2, c2, zs, quotient(xs, 2))
+        return brick, self.c * 8 + self.y * 2 + rest(xs, 2)
 
 
 def coeffs(labels, index, table):
@@ -151,6 +153,49 @@
     me = Place()
     slab_rows = seis_levels.shape[1]
 
+    barrier = pltpu.get_barrier_semaphore()
+
+    def greet(device):
+        pl.semaphore_signal(barrier, inc=1, device_id=device, device_id_type=MESH)
+
+    for dz in range(1, 4):
+        greet(me.device((me.z + dz) % 4, me.xh, me.c, me.y, me.xl))
+
+    @pl.when(me.mid == 0)
+    def _():
+        for z2 in range(4):
+            greet(me.device(z2, 1 - me.xh, me.c, me.y, 1 - me.xl))
+
+    for far in range(2):
+        x2 = 3 * me.xh if far else 1 + me.xl
+        for y2 in range(4):
+            for c2 in range(2):
+                device = me.device(me.z, x2 // 2, c2, y2, x2 % 2)
+                if far:
+
+                    @pl.when(jnp.logical_not(me.is_me(device)))
+                    def _():
+                        greet(device)
+
+                else:
+                    greet(device)
+
+    has_low_x, has_high_x = me.w > 0, me.w < 15
+    has_low_y, has_high_y = me.n > 0, me.n < 7
+    low_x, high_x = (me.w - 1, me.n), (me.w + 1, me.n)
+    low_y, high_y = (me.w, me.n - 1), (me.w, me.n + 1)
+    sides = ((has_low_x, low_x), (has_high_x, high_x), (has_low_y, low_y), (has_high_y, high_y))
+    corners = [
+        (both(sides[sx][0], sides[2 + sy][0]), (me.w + 2 * sx - 1, me.n + 2 * sy - 1))
+        for sx in range(2)
+        for sy in range(2)
+    ]
+    for here, device in (*sides, *corners):
+
+        @pl.when(here)
+        def _():
+            greet(device)
+
     loads = []
     for number, (source, target) in enumerate(
         [
@@ -168,49 +213,6 @@
         copy = pltpu.make_async_copy(source, target, load_sem.at[number])
         copy.start()
         loads.append(copy)
-
-    barrier = pltpu.get_barrier_semaphore()
-
-    def greet(device):
-        pl.semaphore_signal(barrier, inc=1, device_id=device, device_id_type=MESH)
-
-    for dz in range(1, 4):
-        greet(me.device((me.z + dz) % 4, me.xh, me.c, me.y, me.xl))
-
-    @pl.when(me.mid == 0)
-    def _():
-        for z2 in range(4):
-            greet(me.device(z2, 1 - me.xh, me.c, me.y, 1 - me.xl))
-
-    for far in range(2):
-        x2 = 3 * me.xh if far else 1 + me.xl
-        for y2 in range(4):
-            for c2 in range(2):
-                device = me.device(me.z, x2 // 2, c2, y2, x2 % 2)
-                if far:
-
-                    @pl.when(jnp.logical_not(me.is_me(device)))
-                    def _():
-                        greet(device)
-
-                else:
-                    greet(device)
-
-    has_low_x, has_high_x = me.w > 0, me.w < 15
-    has_low_y, has_high_y = me.n > 0, me.n < 7
-    low_x, high_x = (me.w - 1, me.n), (me.w + 1, me.n)
-    low_y, high_y = (me.w, me.n - 1), (me.w, me.n + 1)
-    sides = ((has_low_x, low_x), (has_high_x, high_x), (has_low_y, low_y), (has_high_y, high_y))
-    corners = [
-        (both(sides[sx][0], sides[2 + sy][0]), (me.w + 2 * sx - 1, me.n + 2 * sy - 1))
-        for sx in range(2)
-        for sy in range(2)
-    ]
-    for here, device in (*sides, *corners):
-
-        @pl.when(here)
-        def _():
-            greet(device)
 
     expected = 3 + 4 * (1 - me.mid) + 15 + me.mid
     for here, _ in (*sides, *corners):
@@ -274,17 +276,30 @@
                 sb[field, i, pl.ds((c2 * 2 + column) * PITCH, PITCH), :] = jnp.where(
                     inside, total, 0.0
                 )
-        start_any(
-            sb.at[field, i], hb.at[field, i], leg1_send.at[field], leg1_recv.at[field, i], relay
-        )
+        mine = me.is_me(relay)
+
+        @pl.when(mine)
+        def _():
+            second_leg(field, i, sb)
+
+        @pl.when(jnp.logical_not(mine))
+        def _():
+            remote(
+                sb.at[field, i], hb.at[field, i], leg1_send.at[field], leg1_recv.at[field, i], relay
+            ).start()
 
     def relay_slab(field, i):
-        await_bytes(hb.at[field, i], leg1_recv.at[field, i])
+        @pl.when(jnp.logical_not(me.is_me(me.first_leg(i)[1])))
+        def _():
+            await_bytes(hb.at[field, i], leg1_recv.at[field, i])
+            second_leg(field, i, hb)
+
+    def second_leg(field, i, held):
         for c2 in range(2):
             brick, slot = me.second_leg(i, c2)
             which = (slot > 0).astype(jnp.int32) + (slot > 14).astype(jnp.int32)
             start_any(
-                hb.at[field, i, pl.ds(c2 * MSG, MSG), :],
+                held.at[field, i, pl.ds(c2 * MSG, MSG), :],
                 brick_slot(field, slot),
                 leg2_send.at[field],
                 leg2_recv.at[field, which],
@@ -376,12 +391,12 @@
 
     loads[6].wait()
 
-    def relay_and_send(i, _):
+    def relay_and_send(i):
         relay_slab(0, i)
         send_slab(1, i)
-        return 0
-
-    lax.fori_loop(0, 8, relay_and_send, 0)
+
+    for i in range(8):
+        relay_and_send(i)
 
     def y_halo(field, side):
         source = rb.at[field, pl.ds((2 + side * (NY - 2)) * PITCH, MSG), :]
@@ -424,11 +439,11 @@
             await_bytes(brick_slot(field, slot), leg2_recv.at[field, slot // 15 * 2])
         y_halo_start(field)
 
-    def relay_second(i, _):
+    def relay_second(i):
         relay_slab(1, i)
-        return 0
-
-    lax.fori_loop(0, 8, relay_second, 0)
+
+    for i in range(8):
+        relay_second(i)
     y_halo_early(0)
 
     for here, _, ref, recv in dens_halos:
@@ -565,17 +580,18 @@
         true = me.n >= 0
         vel_columns(field, [1, 2, NY + 1, NY + 2], [me.n > 0, true, true, me.n < 7])
 
-        def back(i, _):
+        def back(i):
             for c2 in range(2):
-                p, slab = me.way_back(i, c2)
+                p = (i * 2 + c2 + 8 * field) % 16
+                slab = (me.n * 2 + p // 8, p % 8)
                 for half in range(2):
                     rs[field, p, pl.ds(half * NX, NX), :] = adjoint(2 * p + 2 + half)
                 start_any(
                     rs.at[field, p], rv.at[field, me.w], ret_send.at[field], ret_recv.at[field], slab
                 )
-            return 0
-
-        lax.fori_loop(0, 8, back, 0)
+
+        for i in range(8):
+            back(i)
 
     def arrive(field):
         await_bytes(rb.at[field, pl.ds(2 * MSG, 14 * MSG), :], leg2_recv.at[field, 1])

time: 50.5 us -> 49.7 us (0.984)
  the two profiles are of different devices: /device:TPU:65 before, /device:TPU:56 now
where the time goes in v6:
time: 49.7 us; the launch traced here: 49.6 us
  Pallas kernels  49 us (99%)
  between operations  0.64 us (1%)
    pallas_call x1, Pallas kernels, shards(): pl.pallas_call(forces_kernel, out_shape=(jax.ShapeDtypeStruct((2, nx, ny,...  45.7 us
    pallas_call x1, Pallas kernels, shards(): pl.pallas_call(functools.partial(chain_kernel, 8), out_shape=(brick_shape...  3.33 us

profile of v6, /device:TPU:56, one launch (start us, length us, event | category | flops | bytes accessed | tf_op | source)
XLA Modules:
  0.0 49.6 jit_solution(14128276866196509410)
XLA Ops:
  0.6 45.7 %forces.1 = (f32[2,32,32,128]{3,2,1,0:T(8,128)S(1)}, f32[2,1024,128]{2,1,0:T(8,128)S(1)}, f32[4,32,32,128]{3,2,1,0:T(8,128)S(1)}, f32[4,1024,128]{2,1,0:T(8,128)S(1)}) custom-call(f32[4,32,32,128]{3,2,1,0:T(8,128)} %grav_levels.1, f32[4,32,32,128]{3,2,1,0:T(8,128)} %grav_step.1, f32[4,1024,128]{2,1,0:T(8,128)} %bitcast.4, f32[4,1024,128]{2,1,0:T(8,128)} %bitcast.5, ...), custom_call_target="tpu_custom_call" | custom-call | tf_op jit(solution)/shard_map/forces/pallas_call | solution.py:738
  46.3 3.3 %chain.1 = (f32[4,32,32,128]{3,2,1,0:T(8,128)}, f32[4,32,32,128]{3,2,1,0:T(8,128)}, f32[4,1024,128]{2,1,0:T(8,128)}, f32[4,1024,128]{2,1,0:T(8,128)}) custom-call(f32[2,32,32,128]{3,2,1,0:T(8,128)S(1)} %get-tuple-element.12.dens_force, f32[2,1024,128]{2,1,0:T(8,128)S(1)} %get-tuple-element.13.vel_force, f32[4,32,32,128]{3,2,1,0:T(8,128)S(1)} %get-tuple-element.14.grav_slope, ...), custom_call_target="tpu_custom_call" | custom-call | tf_op jit(solution)/shard_map/chain/pallas_call | solution.py:797

commit v7 on v6

--- a/solution.py
+++ b/solution.py
@@ -582,8 +582,9 @@
 
         def back(i):
             for c2 in range(2):
-                p = (i * 2 + c2 + 8 * field) % 16
-                slab = (me.n * 2 + p // 8, p % 8)
+                k = i * 2 + c2
+                half_of = rest(me.c + k // 8 + field, 2)
+                p, slab = half_of * 8 + k % 8, (me.n * 2 + half_of, k % 8)
                 for half in range(2):
                     rs[field, p, pl.ds(half * NX, NX), :] = adjoint(2 * p + 2 + half)
                 start_any(

time: 49.7 us -> 49.7 us (level)
  no operation moved by 1% of the time
where the time goes in v7:
time: 49.7 us; the launch traced here: 49.6 us
  Pallas kernels  49 us (99%)
  between operations  0.64 us (1%)
    pallas_call x1, Pallas kernels, shards(): pl.pallas_call(forces_kernel, out_shape=(jax.ShapeDtypeStruct((2, nx, ny,...  45.7 us
    pallas_call x1, Pallas kernels, shards(): pl.pallas_call(functools.partial(chain_kernel, 8), out_shape=(brick_shape...  3.33 us

profile of v7, /device:TPU:56, one launch (start us, length us, event | category | flops | bytes accessed | tf_op | source)
XLA Modules:
  0.0 49.6 jit_solution(5150449513743374531)
XLA Ops:
  0.6 45.7 %forces.1 = (f32[2,32,32,128]{3,2,1,0:T(8,128)S(1)}, f32[2,1024,128]{2,1,0:T(8,128)S(1)}, f32[4,32,32,128]{3,2,1,0:T(8,128)S(1)}, f32[4,1024,128]{2,1,0:T(8,128)S(1)}) custom-call(f32[4,32,32,128]{3,2,1,0:T(8,128)} %grav_levels.1, f32[4,32,32,128]{3,2,1,0:T(8,128)} %grav_step.1, f32[4,1024,128]{2,1,0:T(8,128)} %bitcast.4, f32[4,1024,128]{2,1,0:T(8,128)} %bitcast.5, ...), custom_call_target="tpu_custom_call" | custom-call | tf_op jit(solution)/shard_map/forces/pallas_call | solution.py:739
  46.3 3.3 %chain.1 = (f32[4,32,32,128]{3,2,1,0:T(8,128)}, f32[4,32,32,128]{3,2,1,0:T(8,128)}, f32[4,1024,128]{2,1,0:T(8,128)}, f32[4,1024,128]{2,1,0:T(8,128)}) custom-call(f32[2,32,32,128]{3,2,1,0:T(8,128)S(1)} %get-tuple-element.12.dens_force, f32[2,1024,128]{2,1,0:T(8,128)S(1)} %get-tuple-element.13.vel_force, f32[4,32,32,128]{3,2,1,0:T(8,128)S(1)} %get-tuple-element.14.grav_slope, ...), custom_call_target="tpu_custom_call" | custom-call | tf_op jit(solution)/shard_map/chain/pallas_call | solution.py:798
